TPU v7x, 32 devices: a whole 2x2x4 slice. The times are simulated.
32 devices in a mesh: tile: 32 (over z, y, x, core), fit: 1.
Axes of the slice: x: 2, y: 2, z: 4, core: 2. Of those that a mesh axis runs over, the one named last changes fastest.
Arguments:
- factors: bfloat16 [32, 128, 128, 128], P('tile', 'fit'), may hold values from -0.21875 to 0.21875
- amplitudes: bfloat16 [64, 128, 128], P('tile'), may hold values from -6 to 6
- left_step: int32 [64, 13], P('tile'), may hold values from -1 to 1
- right_step: int32 [64, 13], P('tile'), may hold values from -1 to 1
- amp_owner: int32 [64, 13], P('tile'), may hold values from 0 to 31, all different within a row; in each aligned block of 2 rows (0 to 1, 2 to 3, ...) no two rows name the same one
- amp_slot: int32 [64, 13], P('tile'), may hold values from 0 to 1
Outputs:
- residual: bfloat16 [64, 128, 128], P('tile', 'fit')
Inputs may be any that keep to these rules, and one draw needn't show every extreme that they name: `amp_owner`: among the 13 terms of the 2 residual tiles of one device, no owner index is named more than 1 times, a bound that some block reaches.
All inputs are finite; a program needn't handle non-finite values.
Results may differ from a plain program's by a relative error of at most 0.0049.
Values may be sent and summed in bfloat16 or wider, within the bound.
No kernel may reach another device: no remote copies, remote signals or barrier semaphores. Data moves between devices by JAX's collectives and lax.ppermute only.
A program may use at most 64 MiB of HBM per device.

v0:
```python
import jax
import jax.numpy as jnp
from jax import lax
from jax.sharding import PartitionSpec as P


def padded(cells, sides, width):
    for axis, dim in sides:
        count = lax.axis_size(axis)
        ends = count - 1
        head = lax.slice_in_dim(cells, 0, width, axis=dim)
        tail = lax.slice_in_dim(cells, cells.shape[dim] - width, cells.shape[dim], axis=dim)
        cells = jnp.concatenate(
            [
                lax.ppermute(tail, axis, [(i, (i + 1) % count) for i in range(ends)]),
                cells,
                lax.ppermute(head, axis, [((i + 1) % count, i) for i in range(ends)]),
            ],
            axis=dim,
        )
    return cells


def body(factors, amplitudes, left_step, right_step, amp_owner, amp_slot):
    tiles = lax.axis_size("tile")
    here = lax.axis_index("tile")
    nz_dev = amplitudes.shape[0]
    width = amplitudes.shape[1]
    terms = left_step.shape[1]
    count = nz_dev * terms
    rims = padded(factors, (("tile", 0),), 1)
    left_pos = jnp.clip(here + left_step.reshape(count), 0, tiles - 1) - here + 1
    right_pos = jnp.clip(here + right_step.reshape(count), 0, tiles - 1) - here + 1
    owners = amp_owner.reshape(count)
    slots = amp_slot.reshape(count)
    wanted = owners * nz_dev + slots
    piece = lax.all_gather(amplitudes, "tile", axis=0, tiled=True)
    rows = piece.shape[0]
    marks = (wanted[:, None] == jnp.arange(rows)[None, :]).astype(jnp.bfloat16)
    picked = jnp.dot(marks, piece.reshape(rows, width * width), preferred_element_type=jnp.float32)
    picked = picked.astype(jnp.bfloat16).reshape(count, width, width)

    def add_term(index, total):
        right_fac = lax.dynamic_index_in_dim(rims, right_pos[index], 0, keepdims=False)
        left_fac = lax.dynamic_index_in_dim(rims, left_pos[index], 0, keepdims=False)
        ampl = lax.dynamic_index_in_dim(picked, index, 0, keepdims=False)
        half = jnp.einsum(
            "cd,pbd->pcb", ampl, right_fac, preferred_element_type=jnp.float32
        ).astype(jnp.bfloat16)
        term = jnp.einsum("pac,pcb->ab", left_fac, half, preferred_element_type=jnp.float32)
        return total.at[index // terms].add(term)

    partial_sums = lax.fori_loop(0, count, add_term, jnp.zeros((nz_dev, width, width), jnp.float32))
    return lax.psum_scatter(partial_sums, "fit", scatter_dimension=1, tiled=True).astype(
        jnp.bfloat16
    )


def solution(mesh):
    return jax.shard_map(
        body,
        mesh=mesh,
        in_specs=(
            P("tile", "fit", None, None),
            P("tile", None, None),
            P("tile", None),
            P("tile", None),
            P("tile", None),
            P("tile", None),
        ),
        out_specs=P("tile", "fit", None),
        check_vma=False,
    )
```

profile of v0, /device:TPU:1, one launch (start us, length us, event | category | flops | bytes accessed | tf_op | source)
XLA Modules:
  0.0 1048.4 jit_solution(2643944009490319855)
XLA Ops:
  7.3 7.3 copy.10
  21.3 80.8 %all-gather.2.cloned.1.call-done = bf16[64,128,128]{2,1,0:T(8,128)(2,1)} async-done(((bf16[2,128,128]{2,1,0:T(8,128)(2,1)}), bf16[64,128,128]{2,1,0:T(8,128)(2,1)}) %all-gather.2.cloned.1.call-update) | async-done | bytes 2097168 | tf_op jit(solution)/shard_map/all_gather | solution.py:37
  105.7 10.1 collective-permute-done
  117.5 9.1 pad_maximum_fusion
  126.6 914.3 %while.16 = (s32[]{:T(128)}, f32[2,128,128]{2,1,0:T(8,128)S(1)}, s32[26]{0:T(128)S(1)}, bf16[3,128,128,128]{1,2,3,0:T(8,128)(2,1)}, s32[26]{0:T(128)S(1)}, /*ind...) while((s32[]{:T(128)}, f32[2,128,128]{2,1,0:T(8,128)S(1)}, ...), condition=%wide.region_2.3_spmd, body=%wide.region_0.2_spmd.sunk | while | flops 1073774592 | bytes 42108268 | solution.py:53
  134.4 7.3 copy.23
  147.1 6.8 copy.24
  156.4 5.4 fusion.45
  169.5 7.3 copy.23
  182.2 6.8 copy.24
  191.5 5.4 fusion.45
  204.7 7.3 copy.23
  217.4 6.8 copy.24
  226.7 5.4 fusion.45
  239.9 7.3 copy.23
  252.6 6.8 copy.24
  275.0 7.3 copy.23
  287.7 6.8 copy.24
  310.2 7.3 copy.23
  322.9 6.8 copy.24
  332.2 5.4 fusion.45
  345.4 7.3 copy.23
  358.1 6.8 copy.24
  367.4 5.4 fusion.45
  380.5 7.3 copy.23
  393.2 6.8 copy.24
  402.5 5.4 fusion.45
  415.7 7.3 copy.23
  428.4 6.8 copy.24
  450.9 7.3 copy.23
  463.6 6.8 copy.24
  486.0 7.3 copy.23
  498.7 6.8 copy.24
  508.0 5.4 fusion.45
  521.2 7.3 copy.23
  533.9 6.8 copy.24
  556.4 7.3 copy.23
  569.1 6.8 copy.24
  591.5 7.3 copy.23
  604.2 6.8 copy.24
  626.7 7.3 copy.23
  639.4 6.8 copy.24
  661.9 7.3 copy.23
  674.6 6.8 copy.24
  697.0 7.3 copy.23
  709.7 6.8 copy.24
  732.2 7.3 copy.23
  744.9 6.8 copy.24
  767.4 7.3 copy.23
  780.1 6.8 copy.24
  802.5 7.3 copy.23
  815.2 6.8 copy.24
  837.7 7.3 copy.23
  850.4 6.8 copy.24
  872.9 7.3 copy.23
  885.6 6.8 copy.24
  908.0 7.3 copy.23
  920.7 6.8 copy.24
  943.2 7.3 copy.23
  955.9 6.8 copy.24
  978.4 7.3 copy.23
  991.1 6.8 copy.24
  1013.5 7.3 copy.23
  1026.2 6.8 copy.24
  (176 shorter events, 430.6 us)
Async XLA Ops:
  6.5 95.6 %all-gather.2.cloned.1.call-start = ((), (), s32[]{:S(2)}) async-start(), calls=%async_computation | async-start | bytes 2162688 | tf_op jit(solution)/shard_map/all_gather | solution.py:37
  7.3 13.8 %copy-start.4 = (s32[2,13]{1,0:T(2,128)S(1)}, s32[2,13]{1,0:T(2,128)}, u32[]{:S(2)}) copy-start(s32[2,13]{1,0:T(2,128)} %param.13) | copy-start | bytes 316
  7.3 13.8 %copy-start.5 = (s32[2,13]{1,0:T(2,128)S(1)}, s32[2,13]{1,0:T(2,128)}, u32[]{:S(2)}) copy-start(s32[2,13]{1,0:T(2,128)} %param.12) | copy-start | bytes 316
  7.3 14.0 %copy-start.2 = (s32[2,13]{1,0:T(2,128)S(1)}, s32[2,13]{1,0:T(2,128)}, u32[]{:S(2)}) copy-start(s32[2,13]{1,0:T(2,128)} %param.15) | copy-start | bytes 316
  7.3 14.0 %copy-start.3 = (s32[2,13]{1,0:T(2,128)S(1)}, s32[2,13]{1,0:T(2,128)}, u32[]{:S(2)}) copy-start(s32[2,13]{1,0:T(2,128)} %param.14) | copy-start | bytes 316
  14.6 101.2 %collective-permute-start = (bf16[1,128,128,128]{1,2,3,0:T(8,128)(2,1)}, bf16[1,128,128,128]{1,2,3,0:T(8,128)(2,1)}, u32[]{:S(2)}, u32[]{:S(2)}) collective-permute-start(bf16[1,128,128,128]{1,2,3,0:T(8,128)(2,1)} %copy.10), channel_id=1, source_target_pairs={{0,1},{1,2},{2,3},{3,4},{4,5},{5,6},{6,7},{7,8},{8,9},{9,10},{10,1... | collective-permute-start | bytes 12582920 | tf_op jit(solution)/shard_map/ppermute | solution.py:15
  19.1 98.3 %collective-permute-start.1 = (bf16[1,128,128,128]{1,2,3,0:T(8,128)(2,1)}, bf16[1,128,128,128]{1,2,3,0:T(8,128)(2,1)}, u32[]{:S(2)}, u32[]{:S(2)}) collective-permute-start(bf16[1,128,128,128]{1,2,3,0:T(8,128)(2,1)} %copy.10), channel_id=1, source_target_pairs={{1,0},{2,1},{3,2},{4,3},{5,4},{6,5},{7,6},{8,7},{9,8},{10,9},{11,1... | collective-permute-start | bytes 12582920 | tf_op jit(solution)/shard_map/ppermute | solution.py:17
  102.1 15.3 %copy-start = (bf16[1,128,128,128]{1,2,3,0:T(8,128)(2,1)S(1)}, bf16[1,128,128,128]{1,2,3,0:T(8,128)(2,1)}, u32[]{:S(2)}) copy-start(bf16[1,128,128,128]{1,2,3,0:T(8,128)(2,1)} %copy.10) | copy-start | bytes 12582916
  105.7 20.9 %copy-start.1 = (s32[3]{0:T(128)S(1)}, s32[3]{0:T(128)}, u32[]{:S(2)}) copy-start(s32[3]{0:T(128)} %constant.137.clone.1) | copy-start | bytes 40
Sparse Core Ops, SparseCore 0:
  10.2 91.8 all-gather.1
where the time goes:
time: 1060 us; the launch traced here: 1050 us
  local copies, waits for them, and re-layouts  528 us (50%)
  matrix products  284 us (27%)
  waiting for transfers between devices  93.3 us (9%)
  loops' own time  92.9 us (9%)
  other arithmetic  30.4 us (3%)
  between operations  13.5 us (1%)
    squeeze x52, local copies, waits for them, and re-layouts, add_term(): lax.dynamic_index_in_dim(rims, right_pos[index], 0, keepdims=False)  312 us
    dot_general x26, local copies, waits for them, and re-layouts, add_term(): jnp.einsum('cd,pbd->pcb', ampl, right_fac, preferred_element_type=jnp.flo...  177 us
    dot_general x26, matrix products, add_term(): jnp.einsum('pac,pcb->ab', left_fac, half, preferred_element_type=jnp.floa...  140 us
    dot_general x26, matrix products, add_term(): jnp.einsum('cd,pbd->pcb', ampl, right_fac, preferred_element_type=jnp.flo...  140 us
    another operation x1, loops' own time, body(): lax.fori_loop(0, count, add_term, jnp.zeros((nz_dev, width, width), jnp.f...  92.9 us
    all_gather x1, waiting for transfers between devices, body(): piece = lax.all_gather(amplitudes, 'tile', axis=0, tiled=True)  80.8 us
  transfers between devices with their start and end apart: 3, of which 3 were waited for; matrix products, arithmetic and copies ran while one was open for 1% of the time, Pallas kernels for 0%

commit v1 on v0

v1 whole, which is shorter than its diff:
```python
import functools

import jax
import jax.numpy as jnp
from jax import lax
from jax.experimental import pallas as pl
from jax.experimental.pallas import tpu as pltpu
from jax.sharding import PartitionSpec as P

GROUP = 8
QUADS = 4
PIECES = 2
ORDER = (0, 3, 1, 2)
ROWS = 16
DEPTH = 16
LIMIT = 32 * 1024 * 1024
SMALL = 6 * 1024 * 1024
VMEM = pl.BlockSpec(memory_space=pltpu.VMEM)
SMEM = pl.BlockSpec(memory_space=pltpu.SMEM)
NT = (((1,), (1,)), ((), ()))
FREE = pl.CostEstimate(flops=0, bytes_accessed=0, transcendentals=0)


def pack_kernel(tiles, *refs):
    *sources, out, rows, amps, left, right, owner, slot, sems = refs
    here = lax.axis_index("tile")
    copies = [
        pltpu.make_async_copy(source, held, sems.at[i])
        for i, (source, held) in enumerate(zip(sources, (amps, left, right, owner, slot)))
    ]
    for copy in copies:
        copy.start()
    nz, w, _ = amps.shape
    terms = owner.shape[1]
    rows[...] = jnp.zeros_like(rows)
    for copy in copies:
        copy.wait()
    left_at = jnp.clip(here + left[...], 0, tiles - 1) - here + 1
    right_at = jnp.clip(here + right[...], 0, tiles - 1) - here + 1
    first = lax.broadcasted_iota(jnp.int32, (nz, terms), 0) * 9
    place = first + left_at * 3 + right_at
    turned = first + jnp.where(left_at == 0, 2, left_at - 1) * 3
    turned = turned + jnp.where(right_at == 0, 2, right_at - 1)
    for i, value in enumerate((owner[...], slot[...], place, turned)):
        rows[i * nz:(i + 1) * nz, 0:terms] = value.astype(jnp.float32)
    for s in range(nz):
        out[0, s * w:(s + 1) * w] = amps[s]
    out[0, nz * w:] = rows[...].astype(out.dtype)


def pack(tiles, *sources):
    nz, w, _ = sources[0].shape
    return pl.pallas_call(
        functools.partial(pack_kernel, tiles),
        out_shape=jax.ShapeDtypeStruct((1, nz * w + ROWS, w), sources[0].dtype),
        in_specs=[pl.BlockSpec(memory_space=pl.ANY)] * len(sources),
        out_specs=VMEM,
        scratch_shapes=[pltpu.VMEM((ROWS, w), jnp.float32)]
        + [pltpu.VMEM(source.shape, source.dtype) for source in sources]
        + [pltpu.SemaphoreType.DMA((len(sources),))],
        compiler_params=pltpu.CompilerParams(vmem_limit_bytes=60 * 1024 * 1024),
        cost_estimate=FREE,
        name="pack",
    )(*sources)


def mix_kernel(terms, layers, where, lists_mine, lists_other, amps, *refs):
    *before, out, acc, rows, lists, sem = refs
    column = 1 if before else 0
    w = amps.shape[2]
    nz = acc.shape[0] // 9
    lines = rows.shape[0] // GROUP
    layer, local, core = where[0], where[1], where[3]

    for n, source in enumerate((lists_mine, lists_other)):
        for i in range(QUADS):
            listed = source[i, nz * w:nz * w + ROWS, :].astype(jnp.float32)
            at = (n * QUADS + i) * lines
            rows[at:at + lines] = listed[:lines].astype(jnp.int32)
    copy = pltpu.make_async_copy(rows, lists, sem)
    copy.start()
    copy.wait()

    for step in range(QUADS):
        total = acc if before else out.at[step]
        total[...] = before[0][step] if before else jnp.zeros_like(acc)
        entry = (core * QUADS + step) ^ local
        row = ((entry & 1) * QUADS + (entry >> 1)) * lines

        def add(i, carry):
            for s in range(nz):
                owner = lists[row + s, i]
                slot = lists[row + nz + s, i]
                place = lists[row + (3 if step == 0 else 2) * nz + s, i]
                away = (owner & (GROUP - 1)) ^ local
                turn = layer - (owner >> 3) + layers
                if layers & (layers - 1) == 0:
                    turn = turn & (layers - 1)
                else:
                    turn = lax.rem(turn, layers)
                part = pl.ds(pl.multiple_of(slot * w, w), w)

                @pl.when((away & 1) == column)
                def _():
                    tile = amps[turn * QUADS + (away >> 1), part, :]
                    total[place] = total[place] + tile.astype(jnp.float32)

            return carry

        lax.fori_loop(0, terms, add, 0)
        if not before:
            continue
        for s in range(nz):
            for l in range(3):
                for r in range(3):
                    out[step, (s * 3 + l) * w:(s * 3 + l + 1) * w, r * w:(r + 1) * w] = acc[
                        (s * 3 + l) * 3 + r
                    ].astype(out.dtype)


def mix(where, mine, other, amps, nz, terms, layers, before=()):
    w = amps.shape[2]
    lines = -(-4 * nz // 8) * 8
    first = jax.ShapeDtypeStruct((QUADS, 9 * nz, w, w), jnp.float32)
    second = jax.ShapeDtypeStruct((QUADS, 3 * w * nz, 3 * w), amps.dtype)
    return pl.pallas_call(
        functools.partial(mix_kernel, terms, layers),
        out_shape=second if before else first,
        in_specs=[SMEM] + [VMEM] * (3 + len(before)),
        out_specs=VMEM,
        scratch_shapes=[
            pltpu.VMEM((9 * nz, w, w), jnp.float32),
            pltpu.VMEM((GROUP * lines, w), jnp.int32),
            pltpu.SMEM((GROUP * lines, w), jnp.int32),
            pltpu.SemaphoreType.DMA,
        ],
        compiler_params=pltpu.CompilerParams(vmem_limit_bytes=SMALL),
        cost_estimate=FREE,
        name="mix",
    )(where, mine, other, amps, *before)


def join_kernel(*refs):
    *pieces, out = refs
    size = pieces[0].shape[0]
    for i, piece in enumerate(pieces):
        out[i * size:(i + 1) * size] = piece[...]


def join(pieces):
    size, *rest = pieces[0].shape
    return pl.pallas_call(
        join_kernel,
        out_shape=jax.ShapeDtypeStruct((len(pieces) * size, *rest), pieces[0].dtype),
        in_specs=[VMEM] * len(pieces),
        out_specs=VMEM,
        cost_estimate=FREE,
        compiler_params=pltpu.CompilerParams(vmem_limit_bytes=SMALL),
        name="join",
    )(*pieces)


def sort_kernel(where, a, b, c, d, own_a, own_d, held, mid, halo):
    quad, core = where[2], where[3]
    for t, (tile, own) in enumerate(((a, own_a), (b, None), (c, None), (d, own_d))):
        at = quad ^ t

        def lay(tile, use):
            for_mid = (at == 0) == (core == 1)

            @pl.when(use)
            def _():
                held[at] = tile[...]

            rim = ((at == 0) | (at == QUADS - 1)) & use

            @pl.when(rim & for_mid)
            def _():
                mid[...] = tile[...]

            @pl.when(rim & jnp.logical_not(for_mid))
            def _():
                halo[...] = tile[...]

        if own is None:
            lay(tile, at >= 0)
        else:
            stays = core * QUADS + at == where[1]
            lay(own, stays)
            lay(tile, jnp.logical_not(stays))


def sort(where, tiles, own):
    kind = jax.ShapeDtypeStruct(tiles[0].shape, tiles[0].dtype)
    return pl.pallas_call(
        sort_kernel,
        out_shape=(jax.ShapeDtypeStruct((QUADS,) + kind.shape, kind.dtype), kind, kind),
        in_specs=[SMEM] + [VMEM] * (QUADS + 2),
        out_specs=(VMEM, VMEM, VMEM),
        compiler_params=pltpu.CompilerParams(vmem_limit_bytes=SMALL),
        cost_estimate=FREE,
        name="sort",
    )(where, *tiles, own[0], own[QUADS - 1])


def products(tiles, weights, acc, nz):
    count, w = tiles[0][0].shape[-3:-1]
    depth = next(d for d in (DEPTH, 8, 4, 2, 1) if count % d == 0)
    pair = 2 if depth % 2 == 0 else 1

    def part(step):
        rows = slice(step * depth, (step + 1) * depth)
        x = jnp.concatenate(
            [ref[lead + (rows,)].reshape(depth * w, w) for ref, lead in tiles], axis=1
        )
        half = lax.dot_general(weights, x, NT, preferred_element_type=jnp.float32)
        half = half.astype(x.dtype)
        total = jnp.zeros((w, nz * w), jnp.float32)
        for p in range(0, depth, pair):
            parts = [slice((p + i) * w, (p + i + 1) * w) for i in range(pair)]
            left = jnp.concatenate([x[one] for one in parts], axis=1)
            right = jnp.concatenate(
                [
                    jnp.concatenate(
                        [half[s * 3 * w:(s + 1) * 3 * w, one] for one in parts], axis=0
                    )
                    for s in range(nz)
                ],
                axis=1,
            )
            total += jnp.dot(left, right, preferred_element_type=jnp.float32)
        return total

    acc[...] = sum(part(step) for step in range(count // depth))


def inner_kernel(where, held, weights, *refs):
    *before, out, acc = refs
    nz, w, _ = out.shape[1:]
    for i in range(QUADS - 2):
        products([(held, (i + t,)) for t in range(3)], weights[i + 1], acc, nz)
        for s in range(nz):
            total = acc[:, s * w:(s + 1) * w]
            out[i, s] = total + before[0][i, s] if before else total


def edge_kernel(kind, has_before, where, held, outside, weights, *refs):
    *refs, acc = refs
    core = where[3]
    last = (1 - core) if kind == "beside" else core
    base = last * (QUADS - 2)
    nz, w = refs[-1].shape[-3], refs[-1].shape[-1]
    tiles = [(held, (base,)), (held, (base + 1,)), (outside, ())]
    products(tiles, weights[last * (QUADS - 1)], acc, nz)

    def total(s):
        value = acc[:, s * w:(s + 1) * w]
        return value + refs[0][s] if has_before else value

    done = refs[1:] if has_before else refs
    if len(done) == 1:
        for s in range(nz):
            done[0][s] = total(s)
        return
    inner, beside, *homes = done
    quad = where[2]
    for v, home in enumerate(homes):
        for k in range(2):
            owner = ((v ^ (quad & 1)) << 1) + k

            @pl.when((owner == 1) | (owner == 2))
            def _():
                home[k] = inner[owner - 1]

            @pl.when(owner == last * (QUADS - 1))
            def _():
                for s in range(nz):
                    home[k, s] = total(s)

            @pl.when(owner == (1 - last) * (QUADS - 1))
            def _():
                home[k] = beside[...]


def ladder(kind, where, held, outside, weights, nz, before=None, done=()):
    w = held.shape[-1]
    before = [] if before is None else [before]
    shape = jax.ShapeDtypeStruct((nz, w, w), jnp.float32)
    if kind == "inner":
        kernel, shape = inner_kernel, jax.ShapeDtypeStruct((2, nz, w, w), jnp.float32)
    else:
        kernel = functools.partial(edge_kernel, kind, len(before) > 0)
    if done:
        shape = [jax.ShapeDtypeStruct((2, nz, w, w), jnp.float32)] * 2
    args = [held] + list(outside) + [weights] + before + list(done)
    return pl.pallas_call(
        kernel,
        out_shape=shape,
        in_specs=[SMEM] + [VMEM] * len(args),
        out_specs=[VMEM] * 2 if done else VMEM,
        scratch_shapes=[pltpu.VMEM((w, nz * w), jnp.float32)],
        compiler_params=pltpu.CompilerParams(vmem_limit_bytes=LIMIT),
        cost_estimate=FREE,
        name=kind,
    )(where, *args)


def body(factors, amplitudes, left_step, right_step, amp_owner, amp_slot):
    tiles = lax.axis_size("tile")
    here = lax.axis_index("tile")
    nz, w, _ = amplitudes.shape
    terms = left_step.shape[1]
    layers = tiles // GROUP
    layer, local = here >> 3, here & (GROUP - 1)
    quad, core = local >> 1, local & 1
    where = jnp.stack([layer, local, quad, core, here, tiles]).astype(jnp.int32)
    count = factors.shape[1] // QUADS
    pieces = PIECES if count % PIECES == 0 else 1
    size = count // pieces

    def send(value, target):
        pairs = []
        for z in range(layers):
            for s in range(GROUP):
                to = target(z, s // 2, s % 2)
                if to is not None and to != (z, s // 2, s % 2):
                    pairs.append((z * GROUP + s, to[0] * GROUP + to[1] * 2 + to[2]))
        return lax.ppermute(value, "tile", pairs)

    def cut(piece, t):
        start = (t ^ (local & 3)) * count + piece * size
        return lax.dynamic_slice_in_dim(factors[0], start, size, axis=0)

    def spread(part, t):
        return send(part, lambda z, q, k: (z, t ^ ((q & 1) * 2 + k), q >> 1))

    def to_core(value):
        return send(value, lambda z, q, k: (z, q, 1 - k))

    load = pack(tiles, amplitudes, left_step, right_step, amp_owner, amp_slot)
    where, load = lax.optimization_barrier((where, load))
    loads = [load] + [send(load, lambda z, q, k: (z, q ^ t, k)) for t in range(1, QUADS)]
    own = [[cut(piece, t) for t in range(QUADS)] for piece in range(pieces)]
    loads, own = lax.optimization_barrier((loads, own))
    parts = [{t: spread(own[0][t], t) for t in ORDER[:2]}]
    load = join(loads)
    turns = [
        send(load, lambda z, q, k: ((z + turn) % layers, q, k)) for turn in range(1, layers)
    ]
    sibling = to_core(load)
    if layers > 1:
        turns[0], sibling, own = lax.optimization_barrier((turns[0], sibling, own))
    for t in ORDER[2:]:
        parts[0][t] = spread(own[0][t], t)
    for piece in range(1, pieces):
        parts.append({t: spread(own[piece][t], t) for t in ORDER})
    mine = join([load] + turns)
    mine, parts[0] = lax.optimization_barrier((mine, parts[0]))
    other = to_core(mine)
    half = mix(where, mine, sibling, mine, nz, terms, layers)
    half, parts[0] = lax.optimization_barrier((half, parts[0]))
    weights = mix(where, mine, other, other, nz, terms, layers, (half,))

    def halves(parts, own):
        held, mid, halo = sort(where, [parts[t] for t in range(QUADS)], own)
        halo = send(
            halo,
            lambda z, q, k: (z + 2 * k - 1, q, 1 - k) if 0 <= z + 2 * k - 1 < layers else None,
        )
        return held, to_core(mid), halo

    held, mid, halo = halves(parts[0], own[0])
    ahead = list(ORDER) if pieces > 1 else []
    for t in ahead[:1]:
        held, parts[1][t] = lax.optimization_barrier((held, parts[1][t]))
    inner = beside = beyond = None
    for piece in range(pieces):
        last = piece == pieces - 1
        inner = ladder("inner", where, held, [], weights, nz, inner)
        mid, inner = lax.optimization_barrier((mid, inner))
        for t in ahead[1:2] if piece == 0 else []:
            mid, parts[1][t] = lax.optimization_barrier((mid, parts[1][t]))
        beside = ladder("beside", where, held, [mid], weights, nz, beside)
        halo, beside = lax.optimization_barrier((halo, beside))
        now, outside = held, halo
        if not last:
            beside, after = lax.optimization_barrier((beside, parts[piece + 1]))
            held, mid, halo = halves(after, own[piece + 1])
            held, outside = lax.optimization_barrier((held, outside))
        beyond = ladder(
            "beyond", where, now, [outside], weights, nz, beyond, (inner, beside) if last else ()
        )
        if not last:
            held, beyond = lax.optimization_barrier((held, beyond))

    stays = (quad >> 1) == core
    pair = jnp.where(stays, beyond[0], 0.0)
    for v in range(2):
        pair = pair + send(beyond[v], lambda z, q, k: (z, 2 * k + (v ^ (q & 1)), q >> 1))
    keep = jnp.where(core == 0, pair[0], pair[1])
    give = jnp.where(core == 0, pair[1], pair[0])
    total = keep + to_core(give)
    return lax.psum_scatter(total, "fit", scatter_dimension=1, tiled=True).astype(jnp.bfloat16)


def solution(mesh):
    return jax.shard_map(
        body,
        mesh=mesh,
        in_specs=(
            P("tile", "fit", None, None),
            P("tile", None, None),
            P("tile", None),
            P("tile", None),
            P("tile", None),
            P("tile", None),
        ),
        out_specs=P("tile", "fit", None),
        check_vma=False,
    )
```

time: 1060 us -> 103 us (0.10); the launches traced: 1050 us -> 103 us
  local copies, waits for them, and re-layouts: 528 us -> 2.79 us
  matrix products: 284 us -> 0 us
  loops' own time: 92.9 us -> 0 us
  waiting for transfers between devices: 93.3 us -> 29.8 us
  Pallas kernels: 0 us -> 33.5 us
  other arithmetic: 30.4 us -> 0.71 us
  starting transfers between devices: 6.42 us -> 35.4 us
  between operations: 13.5 us -> 0.31 us
    squeeze x52 -> x0, local copies, waits for them, and re-layouts: 312 us -> none  [add_term(): lax.dynamic_index_in_dim(rims, right_pos[index], 0, keepdims=False)]
    dot_general x53 -> x0, matrix products: 284 us -> none  [the longest x26 140 us: add_term(): jnp.einsum('pac,pcb->ab', left_fac, half, preferred_element_type=jnp.floa...]
    dot_general x26 -> x0, local copies, waits for them, and re-layouts: 177 us -> none  [add_term(): jnp.einsum('cd,pbd->pcb', ampl, right_fac, preferred_element_type=jnp.flo...]
    another operation x1 -> x0, loops' own time: 92.9 us -> none  [body(): lax.fori_loop(0, count, add_term, jnp.zeros((nz_dev, width, width), jnp.f...]
    all_gather x1 -> x0, waiting for transfers between devices: 80.8 us -> none  [body(): piece = lax.all_gather(amplitudes, 'tile', axis=0, tiled=True)]
    pallas_call x0 -> x13, Pallas kernels: none -> 33.5 us  [the longest x6 22.1 us: ladder(): pl.pallas_call(kernel, out_shape=shape, in_specs=[SMEM] + [VMEM] * len(ar...]
    ppermute x2 -> x23, starting transfers between devices: 6.42 us -> 35.4 us  [send(): return lax.ppermute(value, 'tile', pairs)]
    dynamic_slice x52 -> x1, local copies, waits for them, and re-layouts: 31 us -> 2.7 us  [cut(): return lax.dynamic_slice_in_dim(factors[0], start, size, axis=0)]
  transfers between devices with their start and end apart: 3 -> 23, of which waited for: 3 -> 8; matrix products, arithmetic and copies ran while one was open for 1% -> 3% of each run, Pallas kernels for 0% -> 27%
where the time goes in v1:
time: 103 us
  starting transfers between devices  35.4 us (34%)
  Pallas kernels  33.5 us (33%)
  waiting for transfers between devices  29.8 us (29%)
  local copies, waits for them, and re-layouts  2.79 us (3%)
    ppermute x23, starting transfers between devices, send(): return lax.ppermute(value, 'tile', pairs)  35.4 us
    ppermute x23, waiting for transfers between devices, send(): return lax.ppermute(value, 'tile', pairs)  29.8 us
    pallas_call x6, Pallas kernels, ladder(): pl.pallas_call(kernel, out_shape=shape, in_specs=[SMEM] + [VMEM] * len(ar...  22.1 us
    pallas_call x2, Pallas kernels, mix(): pl.pallas_call(functools.partial(mix_kernel, terms, layers), out_shape=se...  8.07 us
    dynamic_slice x1, local copies, waits for them, and re-layouts, cut(): return lax.dynamic_slice_in_dim(factors[0], start, size, axis=0)  2.7 us
  transfers between devices with their start and end apart: 23, of which 8 were waited for; matrix products, arithmetic and copies ran while one was open for 3% of the time, Pallas kernels for 27%

profile of v1, /device:TPU:1, one launch (start us, length us, event | category | flops | bytes accessed | tf_op | source)
XLA Modules:
  0.0 102.5 jit_solution(18319641902646804101)
XLA Ops:
  0.0 1.5 %pack.1.refs_0_ = bf16[1,272,128]{2,1,0:T(8,128)(2,1)} custom-call(bf16[2,128,128]{2,1,0:T(8,128)(2,1)} %refs_0_.1, s32[2,13]{1,0:T(2,128)} %refs_1_.1, s32[2,13]{1,0:T(2,128)} %refs_2_.1, s32[2,13]{1,0:T(2,128)} %refs_3_.1, s32[2,13]{1,0:T(2,128)} %refs_4_.1), custom_call_target="tpu_custom_call" | custom-call | tf_op jit(solution)/shard_map/pack/pallas_call | solution.py:53
  1.5 0.1 stack.23.where
  1.6 2.0 %collective-permute-start = (bf16[1,272,128]{2,1,0:T(8,128)(2,1)}, bf16[1,272,128]{2,1,0:T(8,128)(2,1)S(1)}, u32[]{:S(2)}, u32[]{:S(2)}) collective-permute-start(bf16[1,272,128]{2,1,0:T(8,128)(2,1)} %pack.1.refs_0_), channel_id=1, source_target_pairs={{0,2},{1,3},{2,0},{3,1},{4,6},{5,7},{6,4},{7,5},{8,10},{9,11},{10,... | collective-permute-start | bytes 208904 | tf_op jit(solution)/shard_map/ppermute | solution.py:328
  3.7 1.2 %collective-permute-start.1 = (bf16[1,272,128]{2,1,0:T(8,128)(2,1)}, bf16[1,272,128]{2,1,0:T(8,128)(2,1)S(1)}, u32[]{:S(2)}, u32[]{:S(2)}) collective-permute-start(bf16[1,272,128]{2,1,0:T(8,128)(2,1)} %pack.1.refs_0_), channel_id=1, source_target_pairs={{0,4},{1,5},{2,6},{3,7},{4,0},{5,1},{6,2},{7,3},{8,12},{9,13},{10,... | collective-permute-start | bytes 208904 | tf_op jit(solution)/shard_map/ppermute | solution.py:328
  4.9 0.0 collective-permute-start.2
  4.9 0.0 copy-start
  4.9 2.7 %dynamic-slice_bitcast_fusion = (bf16[16,128,128]{2,1,0:T(8,128)(2,1)S(1)}, bf16[16,128,128]{2,1,0:T(8,128)(2,1)S(1)}, bf16[16,128,128]{2,1,0:T(8,128)(2,1)S(1)}...) fusion(bf16[1,128,128,128]{3,2,1,0:T(8,128)(2,1)} %param.6, ...), kind=kLoop, calls=%fused_computation | loop fusion | bytes 8388640 | tf_op jit(solution)/shard_map/dynamic_slice | solution.py:332
  7.6 0.0 collective-permute-done.refs_1_
  7.6 0.0 collective-permute-done.1.refs_2_
  7.7 1.5 %collective-permute-done.2.refs_3_ = bf16[1,272,128]{2,1,0:T(8,128)(2,1)S(1)} collective-permute-done((bf16[1,272,128]{2,1,0:T(8,128)(2,1)}, bf16[1,272,128]{2,1,0:T(8,128)(2,1)S(1)}, u32[]{:S(2)}, u32[]{:S(2)}) %collective-permute-start.2) | collective-permute-done | bytes 69664 | tf_op jit(solution)/shard_map/ppermute | solution.py:328
  9.2 0.0 copy-done
  9.2 1.3 %collective-permute-start.3 = (bf16[4,272,128]{2,1,0:T(8,128)(2,1)S(1)}, bf16[4,272,128]{2,1,0:T(8,128)(2,1)S(1)}, u32[]{:S(2)}, u32[]{:S(2)}) collective-permute-start(bf16[4,272,128]{2,1,0:T(8,128)(2,1)S(1)} %join.2.refs_0_), channel_id=1, source_target_pairs={{0,8},{1,9},{2,10},{3,11},{4,12},{5,13},{6,14},{7,15},{8,16},{9,17... | collective-permute-start | bytes 835592 | tf_op jit(solution)/shard_map/ppermute | solution.py:328
  10.6 2.6 %collective-permute-start.4 = (bf16[4,272,128]{2,1,0:T(8,128)(2,1)S(1)}, bf16[4,272,128]{2,1,0:T(8,128)(2,1)S(1)}, u32[]{:S(2)}, u32[]{:S(2)}) collective-permute-start(bf16[4,272,128]{2,1,0:T(8,128)(2,1)S(1)} %join.2.refs_0_), channel_id=1, source_target_pairs={{0,1},{1,0},{2,3},{3,2},{4,5},{5,4},{6,7},{7,6},{8,9},{9,8},{10,11... | collective-permute-start | bytes 835592 | tf_op jit(solution)/shard_map/ppermute | solution.py:328
  13.2 2.3 %collective-permute-start.5 = (bf16[4,272,128]{2,1,0:T(8,128)(2,1)S(1)}, bf16[4,272,128]{2,1,0:T(8,128)(2,1)S(1)}, u32[]{:S(2)}, u32[]{:S(2)}) collective-permute-start(bf16[4,272,128]{2,1,0:T(8,128)(2,1)S(1)} %join.2.refs_0_), channel_id=1, source_target_pairs={{0,16},{1,17},{2,18},{3,19},{4,20},{5,21},{6,22},{7,23},{8,24},{9,... | collective-permute-start | bytes 835592 | tf_op jit(solution)/shard_map/ppermute | solution.py:328
  15.5 2.3 %collective-permute-start.10 = (bf16[16,128,128]{2,1,0:T(8,128)(2,1)S(1)}, bf16[16,128,128]{2,1,0:T(8,128)(2,1)S(1)}, u32[]{:S(2)}, u32[]{:S(2)}) collective-permute-start(bf16[16,128,128]{2,1,0:T(8,128)(2,1)S(1)} %get-tuple-element.96.own_d), channel_id=1, source_target_pairs={{0,6},{1,4},{3,0},{4,7},{6,3},{7,1},{8,14},{9,12},{11,8},{12,15},{... | collective-permute-start | bytes 1572872 | tf_op jit(solution)/shard_map/ppermute | solution.py:328
  17.8 1.9 %collective-permute-start.7 = (bf16[16,128,128]{2,1,0:T(8,128)(2,1)S(1)}, bf16[16,128,128]{2,1,0:T(8,128)(2,1)S(1)}, u32[]{:S(2)}, u32[]{:S(2)}) collective-permute-start(bf16[16,128,128]{2,1,0:T(8,128)(2,1)S(1)} %get-tuple-element.95.own_a), channel_id=1, source_target_pairs={{1,2},{2,4},{3,6},{4,1},{5,3},{6,5},{9,10},{10,12},{11,14},{12,9},... | collective-permute-start | bytes 1572872 | tf_op jit(solution)/shard_map/ppermute | solution.py:328
  19.8 0.0 collective-permute-done.3.refs_1_
  19.8 0.0 collective-permute-done.4.lists_other
  19.8 2.5 %collective-permute-start.8 = (bf16[16,128,128]{2,1,0:T(8,128)(2,1)S(1)}, bf16[16,128,128]{2,1,0:T(8,128)(2,1)S(1)}, u32[]{:S(2)}, u32[]{:S(2)}) collective-permute-start(bf16[16,128,128]{2,1,0:T(8,128)(2,1)S(1)} %get-tuple-element.83), channel_id=1, source_target_pairs={{0,2},{1,0},{2,6},{3,4},{4,3},{5,1},{6,7},{7,5},{8,10},{9,8},{10,1... | collective-permute-start | bytes 1572872 | tf_op jit(solution)/shard_map/ppermute | solution.py:328
  22.3 0.8 collective-permute-start.9
  23.1 8.6 %collective-permute-done.5.refs_2_ = bf16[4,272,128]{2,1,0:T(8,128)(2,1)S(1)} collective-permute-done((bf16[4,272,128]{2,1,0:T(8,128)(2,1)S(1)}, bf16[4,272,128]{2,1,0:T(8,128)(2,1)S(1)}, u32[]{:S(2)}, u32[]{:S(2)}) %collective-permute-start.5) | collective-permute-done | bytes 278560 | tf_op jit(solution)/shard_map/ppermute | solution.py:328
  31.7 0.0 collective-permute-start.6
  31.7 7.8 %collective-permute-done.6.refs_3_ = bf16[4,272,128]{2,1,0:T(8,128)(2,1)S(1)} collective-permute-done((bf16[4,272,128]{2,1,0:T(8,128)(2,1)S(1)}, bf16[4,272,128]{2,1,0:T(8,128)(2,1)S(1)}, u32[]{:S(2)}, u32[]{:S(2)}) %collective-permute-start.6) | collective-permute-done | bytes 278560 | tf_op jit(solution)/shard_map/ppermute | solution.py:328
  39.5 0.1 join.3.lists_mine.amps
  39.6 0.0 collective-permute-done.10.d
  39.6 2.1 %collective-permute-done.7.a = bf16[16,128,128]{2,1,0:T(8,128)(2,1)S(1)} collective-permute-done((bf16[16,128,128]{2,1,0:T(8,128)(2,1)S(1)}, bf16[16,128,128]{2,1,0:T(8,128)(2,1)S(1)}, u32[]{:S(2)}, u32[]{:S(2)}) %collective-permute-start.7) | collective-permute-done | bytes 524320 | tf_op jit(solution)/shard_map/ppermute | solution.py:328
  41.7 1.7 %collective-permute-done.8.b = bf16[16,128,128]{2,1,0:T(8,128)(2,1)S(1)} collective-permute-done((bf16[16,128,128]{2,1,0:T(8,128)(2,1)S(1)}, bf16[16,128,128]{2,1,0:T(8,128)(2,1)S(1)}, u32[]{:S(2)}, u32[]{:S(2)}) %collective-permute-start.8) | collective-permute-done | bytes 524320 | tf_op jit(solution)/shard_map/ppermute | solution.py:328
  43.4 0.0 collective-permute-done.9.c
  43.4 0.0 collective-permute-start.14
  43.4 2.0 %collective-permute-start.12 = (bf16[16,128,128]{2,1,0:T(8,128)(2,1)S(1)}, bf16[16,128,128]{2,1,0:T(8,128)(2,1)S(1)}, u32[]{:S(2)}, u32[]{:S(2)}) collective-permute-start(bf16[16,128,128]{2,1,0:T(8,128)(2,1)S(1)} %get-tuple-element.99.own_a), channel_id=1, source_target_pairs={{1,2},{2,4},{3,6},{4,1},{5,3},{6,5},{9,10},{10,12},{11,14},{12,9},... | collective-permute-start | bytes 1572872 | tf_op jit(solution)/shard_map/ppermute | solution.py:328
  45.4 3.9 %mix.2.refs_0_ = f32[4,18,128,128]{3,2,1,0:T(8,128)S(1)} custom-call(s32[6]{0:T(128)S(1)} %stack.23.where, bf16[16,272,128]{2,1,0:T(8,128)(2,1)S(1)} %join.3.lists_mine.amps, bf16[4,272,128]{2,1,0:T(8,128)(2,1)S(1)} %collective-permute-done.4.lists_other, bf16[16,272,128]{2,1,0:T(8,128)(2,1)S(1)} %join.3.lists_mine.amps), custom_call_target="tpu_custom_call" | custom-call | tf_op jit(solution)/shard_map/mix/pallas_call | solution.py:126
  49.3 0.8 sort.2
  50.1 0.1 collective-permute-start.13
  50.2 3.5 %collective-permute-start.15 = (bf16[16,128,128]{2,1,0:T(8,128)(2,1)S(1)}, bf16[16,128,128]{2,1,0:T(8,128)(2,1)S(1)}, u32[]{:S(2)}, u32[]{:S(2)}) collective-permute-start(bf16[16,128,128]{2,1,0:T(8,128)(2,1)S(1)} %get-tuple-element.104.own_d), channel_id=1, source_target_pairs={{0,6},{1,4},{3,0},{4,7},{6,3},{7,1},{8,14},{9,12},{11,8},{12,15},{... | collective-permute-start | bytes 1572872 | tf_op jit(solution)/shard_map/ppermute | solution.py:328
  53.7 2.8 %collective-permute-start.11 = (bf16[16,128,128]{2,1,0:T(8,128)(2,1)S(1)}, bf16[16,128,128]{2,1,0:T(8,128)(2,1)S(1)}, u32[]{:S(2)}, u32[]{:S(2)}) collective-permute-start(bf16[16,128,128]{2,1,0:T(8,128)(2,1)S(1)} %get-tuple-element.97), channel_id=1, source_target_pairs={{1,8},{3,10},{5,12},{7,14},{8,1},{9,16},{10,3},{11,18},{12,5},{13,... | collective-permute-start | bytes 1572872 | tf_op jit(solution)/shard_map/ppermute | solution.py:328
  56.6 0.0 collective-permute-done.12.a
  56.6 0.1 collective-permute-start.16
  56.6 0.0 collective-permute-done.14.lists_other.amps
  56.7 1.5 %collective-permute-start.17 = (bf16[16,128,128]{2,1,0:T(8,128)(2,1)S(1)}, bf16[16,128,128]{2,1,0:T(8,128)(2,1)S(1)}, u32[]{:S(2)}, u32[]{:S(2)}) collective-permute-start(bf16[16,128,128]{2,1,0:T(8,128)(2,1)S(1)} %get-tuple-element.109), channel_id=1, source_target_pairs={{0,4},{1,6},{2,0},{3,2},{4,5},{5,7},{6,1},{7,3},{8,12},{9,14},{10,... | collective-permute-start | bytes 1572872 | tf_op jit(solution)/shard_map/ppermute | solution.py:328
  58.2 4.2 %mix.3.weights = bf16[4,768,384]{2,1,0:T(8,128)(2,1)S(1)} custom-call(s32[6]{0:T(128)S(1)} %stack.23.where, bf16[16,272,128]{2,1,0:T(8,128)(2,1)S(1)} %join.3.lists_mine.amps, bf16[16,272,128]{2,1,0:T(8,128)(2,1)S(1)} %collective-permute-done.14.lists_other.amps, bf16[16,272,128]{2,1,0:T(8,128)(2,1)S(1)} %collective-permute-done.14.lists_other.amps, ...), custom_call_target="tpu_custom_call" | custom-call | tf_op jit(solution)/shard_map/mix/pallas_call | solution.py:126
  62.4 5.0 %inner.2.refs_0_ = f32[2,2,128,128]{3,2,1,0:T(8,128)S(1)} custom-call(s32[6]{0:T(128)S(1)} %stack.23.where, bf16[4,16,128,128]{3,2,1,0:T(8,128)(2,1)S(1)} %get-tuple-element.100.held, bf16[4,768,384]{2,1,0:T(8,128)(2,1)S(1)} %mix.3.weights), custom_call_target="tpu_custom_call" | custom-call | tf_op jit(solution)/shard_map/inner/pallas_call | solution.py:296
  67.4 0.0 collective-permute-done.13.outside
  67.4 0.0 collective-permute-done.15.d
  67.5 3.0 %beside.2.refs_0_ = f32[2,128,128]{2,1,0:T(8,128)S(1)} custom-call(s32[6]{0:T(128)S(1)} %stack.23.where, bf16[4,16,128,128]{3,2,1,0:T(8,128)(2,1)S(1)} %get-tuple-element.100.held, bf16[16,128,128]{2,1,0:T(8,128)(2,1)S(1)} %collective-permute-done.13.outside, bf16[4,768,384]{2,1,0:T(8,128)(2,1)S(1)} %mix.3.weights), custom_call_target="tpu_custom_call" | custom-call | tf_op jit(solution)/shard_map/beside/pallas_call | solution.py:296
  70.5 0.0 collective-permute-done.11.outside
  70.5 1.8 %collective-permute-done.16.b = bf16[16,128,128]{2,1,0:T(8,128)(2,1)S(1)} collective-permute-done((bf16[16,128,128]{2,1,0:T(8,128)(2,1)S(1)}, bf16[16,128,128]{2,1,0:T(8,128)(2,1)S(1)}, u32[]{:S(2)}, u32[]{:S(2)}) %collective-permute-start.16) | collective-permute-done | bytes 524320 | tf_op jit(solution)/shard_map/ppermute | solution.py:328
  72.3 0.0 collective-permute-done.17.c
  72.3 0.8 sort.3
  73.1 0.1 collective-permute-start.19
  73.2 2.5 %collective-permute-start.18 = (bf16[16,128,128]{2,1,0:T(8,128)(2,1)S(1)}, bf16[16,128,128]{2,1,0:T(8,128)(2,1)S(1)}, u32[]{:S(2)}, u32[]{:S(2)}) collective-permute-start(bf16[16,128,128]{2,1,0:T(8,128)(2,1)S(1)} %get-tuple-element.120), channel_id=1, source_target_pairs={{1,8},{3,10},{5,12},{7,14},{8,1},{9,16},{10,3},{11,18},{12,5},{13,... | collective-permute-start | bytes 1572872 | tf_op jit(solution)/shard_map/ppermute | solution.py:328
  75.7 3.0 %beyond.2.refs_0_ = f32[2,128,128]{2,1,0:T(8,128)S(1)} custom-call(s32[6]{0:T(128)S(1)} %stack.23.where, bf16[4,16,128,128]{3,2,1,0:T(8,128)(2,1)S(1)} %get-tuple-element.100.held, bf16[16,128,128]{2,1,0:T(8,128)(2,1)S(1)} %collective-permute-done.11.outside, bf16[4,768,384]{2,1,0:T(8,128)(2,1)S(1)} %mix.3.weights), custom_call_target="tpu_custom_call" | custom-call | tf_op jit(solution)/shard_map/beyond/pallas_call | solution.py:296
  78.7 5.0 %inner.3.refs_1_ = f32[2,2,128,128]{3,2,1,0:T(8,128)S(1)} custom-call(s32[6]{0:T(128)S(1)} %stack.23.where, bf16[4,16,128,128]{3,2,1,0:T(8,128)(2,1)S(1)} %get-tuple-element.119.held, bf16[4,768,384]{2,1,0:T(8,128)(2,1)S(1)} %mix.3.weights, f32[2,2,128,128]{3,2,1,0:T(8,128)S(1)} %inner.2.refs_0_), custom_call_target="tpu_custom_call" | custom-call | tf_op jit(solution)/shard_map/inner/pallas_call | solution.py:296
  83.8 0.0 collective-permute-done.19.outside
  83.8 3.0 %beside.3.refs_2_ = f32[2,128,128]{2,1,0:T(8,128)S(1)} custom-call(s32[6]{0:T(128)S(1)} %stack.23.where, bf16[4,16,128,128]{3,2,1,0:T(8,128)(2,1)S(1)} %get-tuple-element.119.held, bf16[16,128,128]{2,1,0:T(8,128)(2,1)S(1)} %collective-permute-done.19.outside, bf16[4,768,384]{2,1,0:T(8,128)(2,1)S(1)} %mix.3.weights, f32[2,128,128]{2,1,0:T(8,128)S(1)} %beside.2.refs_0_), custom_call_target="tpu_custom_call" | custom-call | tf_op jit(solution)/shard_map/beside/pallas_call | solution.py:296
  86.8 0.0 collective-permute-done.18.outside
  86.8 3.1 %beyond.3 = (f32[2,2,128,128]{3,2,1,0:T(8,128)S(1)}, f32[2,2,128,128]{3,2,1,0:T(8,128)S(1)}) custom-call(s32[6]{0:T(128)S(1)} %stack.23.where, bf16[4,16,128,128]{3,2,1,0:T(8,128)(2,1)S(1)} %get-tuple-element.119.held, bf16[16,128,128]{2,1,0:T(8,128)(2,1)S(1)} %collective-permute-done.18.outside, bf16[4,768,384]{2,1,0:T(8,128)(2,1)S(1)} %mix.3.weights, ...), custom_call_target="tpu_custom_call" | custom-call | tf_op jit(solution)/shard_map/beyond/pallas_call | solution.py:296
  89.9 1.9 %collective-permute-start.20 = (f32[2,2,128,128]{3,2,1,0:T(8,128)S(1)}, f32[2,2,128,128]{3,2,1,0:T(8,128)S(1)}, u32[]{:S(2)}, u32[]{:S(2)}) collective-permute-start(f32[2,2,128,128]{3,2,1,0:T(8,128)S(1)} %get-tuple-element.129), channel_id=1, source_target_pairs={{1,4},{3,6},{4,1},{6,3},{9,12},{11,14},{12,9},{14,11},{17,20},{19,... | collective-permute-start | bytes 786440 | tf_op jit(solution)/shard_map/ppermute | solution.py:328
  91.8 3.6 %collective-permute-start.21 = (f32[2,2,128,128]{3,2,1,0:T(8,128)S(1)}, f32[2,2,128,128]{3,2,1,0:T(8,128)S(1)}, u32[]{:S(2)}, u32[]{:S(2)}) collective-permute-start(f32[2,2,128,128]{3,2,1,0:T(8,128)S(1)} %get-tuple-element.130), channel_id=1, source_target_pairs={{0,2},{1,6},{2,0},{3,4},{4,3},{5,7},{6,1},{7,5},{8,10},{9,14},{10,... | collective-permute-start | bytes 786440 | tf_op jit(solution)/shard_map/ppermute | solution.py:328
  95.4 5.0 %collective-permute-done.20 = f32[2,2,128,128]{3,2,1,0:T(8,128)S(1)} collective-permute-done((f32[2,2,128,128]{3,2,1,0:T(8,128)S(1)}, f32[2,2,128,128]{3,2,1,0:T(8,128)S(1)}, u32[]{:S(2)}, u32[]{:S(2)}) %collective-permute-start.20) | collective-permute-done | bytes 262176 | tf_op jit(solution)/shard_map/ppermute | solution.py:328
  100.4 0.0 collective-permute-done.21
  100.5 0.1 collective-permute-start.22
  100.6 1.3 %collective-permute-done.22 = f32[2,128,128]{2,1,0:T(8,128)S(1)} collective-permute-done((f32[2,128,128]{2,1,0:T(8,128)S(1)}, f32[2,128,128]{2,1,0:T(8,128)S(1)}, u32[]{:S(2)}, u32[]{:S(2)}) %collective-permute-start.22) | collective-permute-done | bytes 131104 | tf_op jit(solution)/shard_map/ppermute | solution.py:328
  101.9 0.7 fusion
  (3 shorter events, 0.1 us)
Async XLA Ops:
  1.6 6.0 %collective-permute-start = (bf16[1,272,128]{2,1,0:T(8,128)(2,1)}, bf16[1,272,128]{2,1,0:T(8,128)(2,1)S(1)}, u32[]{:S(2)}, u32[]{:S(2)}) collective-permute-start(bf16[1,272,128]{2,1,0:T(8,128)(2,1)} %pack.1.refs_0_), channel_id=1, source_target_pairs={{0,2},{1,3},{2,0},{3,1},{4,6},{5,7},{6,4},{7,5},{8,10},{9,11},{10,... | collective-permute-start | bytes 208904 | tf_op jit(solution)/shard_map/ppermute | solution.py:328
  3.7 4.0 %collective-permute-start.1 = (bf16[1,272,128]{2,1,0:T(8,128)(2,1)}, bf16[1,272,128]{2,1,0:T(8,128)(2,1)S(1)}, u32[]{:S(2)}, u32[]{:S(2)}) collective-permute-start(bf16[1,272,128]{2,1,0:T(8,128)(2,1)} %pack.1.refs_0_), channel_id=1, source_target_pairs={{0,4},{1,5},{2,6},{3,7},{4,0},{5,1},{6,2},{7,3},{8,12},{9,13},{10,... | collective-permute-start | bytes 208904 | tf_op jit(solution)/shard_map/ppermute | solution.py:328
  4.9 4.3 %collective-permute-start.2 = (bf16[1,272,128]{2,1,0:T(8,128)(2,1)}, bf16[1,272,128]{2,1,0:T(8,128)(2,1)S(1)}, u32[]{:S(2)}, u32[]{:S(2)}) collective-permute-start(bf16[1,272,128]{2,1,0:T(8,128)(2,1)} %pack.1.refs_0_), channel_id=1, source_target_pairs={{0,6},{1,7},{2,4},{3,5},{4,2},{5,3},{6,0},{7,1},{8,14},{9,15},{10,... | collective-permute-start | bytes 208904 | tf_op jit(solution)/shard_map/ppermute | solution.py:328
  4.9 4.3 %copy-start = (bf16[1,272,128]{2,1,0:T(8,128)(2,1)S(1)}, bf16[1,272,128]{2,1,0:T(8,128)(2,1)}, u32[]{:S(2)}) copy-start(bf16[1,272,128]{2,1,0:T(8,128)(2,1)} %pack.1.refs_0_) | copy-start | bytes 208900
  9.2 10.5 %collective-permute-start.3 = (bf16[4,272,128]{2,1,0:T(8,128)(2,1)S(1)}, bf16[4,272,128]{2,1,0:T(8,128)(2,1)S(1)}, u32[]{:S(2)}, u32[]{:S(2)}) collective-permute-start(bf16[4,272,128]{2,1,0:T(8,128)(2,1)S(1)} %join.2.refs_0_), channel_id=1, source_target_pairs={{0,8},{1,9},{2,10},{3,11},{4,12},{5,13},{6,14},{7,15},{8,16},{9,17... | collective-permute-start | bytes 835592 | tf_op jit(solution)/shard_map/ppermute | solution.py:328
  10.6 9.2 %collective-permute-start.4 = (bf16[4,272,128]{2,1,0:T(8,128)(2,1)S(1)}, bf16[4,272,128]{2,1,0:T(8,128)(2,1)S(1)}, u32[]{:S(2)}, u32[]{:S(2)}) collective-permute-start(bf16[4,272,128]{2,1,0:T(8,128)(2,1)S(1)} %join.2.refs_0_), channel_id=1, source_target_pairs={{0,1},{1,0},{2,3},{3,2},{4,5},{5,4},{6,7},{7,6},{8,9},{9,8},{10,11... | collective-permute-start | bytes 835592 | tf_op jit(solution)/shard_map/ppermute | solution.py:328
  13.2 18.5 %collective-permute-start.5 = (bf16[4,272,128]{2,1,0:T(8,128)(2,1)S(1)}, bf16[4,272,128]{2,1,0:T(8,128)(2,1)S(1)}, u32[]{:S(2)}, u32[]{:S(2)}) collective-permute-start(bf16[4,272,128]{2,1,0:T(8,128)(2,1)S(1)} %join.2.refs_0_), channel_id=1, source_target_pairs={{0,16},{1,17},{2,18},{3,19},{4,20},{5,21},{6,22},{7,23},{8,24},{9,... | collective-permute-start | bytes 835592 | tf_op jit(solution)/shard_map/ppermute | solution.py:328
  15.5 24.1 %collective-permute-start.10 = (bf16[16,128,128]{2,1,0:T(8,128)(2,1)S(1)}, bf16[16,128,128]{2,1,0:T(8,128)(2,1)S(1)}, u32[]{:S(2)}, u32[]{:S(2)}) collective-permute-start(bf16[16,128,128]{2,1,0:T(8,128)(2,1)S(1)} %get-tuple-element.96.own_d), channel_id=1, source_target_pairs={{0,6},{1,4},{3,0},{4,7},{6,3},{7,1},{8,14},{9,12},{11,8},{12,15},{... | collective-permute-start | bytes 1572872 | tf_op jit(solution)/shard_map/ppermute | solution.py:328
  17.8 23.9 %collective-permute-start.7 = (bf16[16,128,128]{2,1,0:T(8,128)(2,1)S(1)}, bf16[16,128,128]{2,1,0:T(8,128)(2,1)S(1)}, u32[]{:S(2)}, u32[]{:S(2)}) collective-permute-start(bf16[16,128,128]{2,1,0:T(8,128)(2,1)S(1)} %get-tuple-element.95.own_a), channel_id=1, source_target_pairs={{1,2},{2,4},{3,6},{4,1},{5,3},{6,5},{9,10},{10,12},{11,14},{12,9},... | collective-permute-start | bytes 1572872 | tf_op jit(solution)/shard_map/ppermute | solution.py:328
  19.8 23.6 %collective-permute-start.8 = (bf16[16,128,128]{2,1,0:T(8,128)(2,1)S(1)}, bf16[16,128,128]{2,1,0:T(8,128)(2,1)S(1)}, u32[]{:S(2)}, u32[]{:S(2)}) collective-permute-start(bf16[16,128,128]{2,1,0:T(8,128)(2,1)S(1)} %get-tuple-element.83), channel_id=1, source_target_pairs={{0,2},{1,0},{2,6},{3,4},{4,3},{5,1},{6,7},{7,5},{8,10},{9,8},{10,1... | collective-permute-start | bytes 1572872 | tf_op jit(solution)/shard_map/ppermute | solution.py:328
  22.3 21.1 %collective-permute-start.9 = (bf16[16,128,128]{2,1,0:T(8,128)(2,1)S(1)}, bf16[16,128,128]{2,1,0:T(8,128)(2,1)S(1)}, u32[]{:S(2)}, u32[]{:S(2)}) collective-permute-start(bf16[16,128,128]{2,1,0:T(8,128)(2,1)S(1)} %get-tuple-element.84), channel_id=1, source_target_pairs={{0,4},{1,6},{2,0},{3,2},{4,5},{5,7},{6,1},{7,3},{8,12},{9,14},{10,... | collective-permute-start | bytes 1572872 | tf_op jit(solution)/shard_map/ppermute | solution.py:328
  31.7 7.8 %collective-permute-start.6 = (bf16[4,272,128]{2,1,0:T(8,128)(2,1)S(1)}, bf16[4,272,128]{2,1,0:T(8,128)(2,1)S(1)}, u32[]{:S(2)}, u32[]{:S(2)}) collective-permute-start(bf16[4,272,128]{2,1,0:T(8,128)(2,1)S(1)} %join.2.refs_0_), channel_id=1, source_target_pairs={{0,24},{1,25},{2,26},{3,27},{4,28},{5,29},{6,30},{7,31},{8,0},{9,1... | collective-permute-start | bytes 835592 | tf_op jit(solution)/shard_map/ppermute | solution.py:328
  43.4 13.3 %collective-permute-start.14 = (bf16[16,272,128]{2,1,0:T(8,128)(2,1)S(1)}, bf16[16,272,128]{2,1,0:T(8,128)(2,1)S(1)}, u32[]{:S(2)}, u32[]{:S(2)}) collective-permute-start(bf16[16,272,128]{2,1,0:T(8,128)(2,1)S(1)} %join.3.lists_mine.amps), channel_id=1, source_target_pairs={{0,1},{1,0},{2,3},{3,2},{4,5},{5,4},{6,7},{7,6},{8,9},{9,8},{10,11... | collective-permute-start | bytes 3342344 | tf_op jit(solution)/shard_map/ppermute | solution.py:328
  43.4 13.2 %collective-permute-start.12 = (bf16[16,128,128]{2,1,0:T(8,128)(2,1)S(1)}, bf16[16,128,128]{2,1,0:T(8,128)(2,1)S(1)}, u32[]{:S(2)}, u32[]{:S(2)}) collective-permute-start(bf16[16,128,128]{2,1,0:T(8,128)(2,1)S(1)} %get-tuple-element.99.own_a), channel_id=1, source_target_pairs={{1,2},{2,4},{3,6},{4,1},{5,3},{6,5},{9,10},{10,12},{11,14},{12,9},... | collective-permute-start | bytes 1572872 | tf_op jit(solution)/shard_map/ppermute | solution.py:328
  50.1 17.3 %collective-permute-start.13 = (bf16[16,128,128]{2,1,0:T(8,128)(2,1)S(1)}, bf16[16,128,128]{2,1,0:T(8,128)(2,1)S(1)}, u32[]{:S(2)}, u32[]{:S(2)}) collective-permute-start(bf16[16,128,128]{2,1,0:T(8,128)(2,1)S(1)} %get-tuple-element.101), channel_id=1, source_target_pairs={{0,1},{1,0},{2,3},{3,2},{4,5},{5,4},{6,7},{7,6},{8,9},{9,8},{10,11... | collective-permute-start | bytes 1572872 | tf_op jit(solution)/shard_map/ppermute | solution.py:328
  50.2 17.2 %collective-permute-start.15 = (bf16[16,128,128]{2,1,0:T(8,128)(2,1)S(1)}, bf16[16,128,128]{2,1,0:T(8,128)(2,1)S(1)}, u32[]{:S(2)}, u32[]{:S(2)}) collective-permute-start(bf16[16,128,128]{2,1,0:T(8,128)(2,1)S(1)} %get-tuple-element.104.own_d), channel_id=1, source_target_pairs={{0,6},{1,4},{3,0},{4,7},{6,3},{7,1},{8,14},{9,12},{11,8},{12,15},{... | collective-permute-start | bytes 1572872 | tf_op jit(solution)/shard_map/ppermute | solution.py:328
  53.7 16.7 %collective-permute-start.11 = (bf16[16,128,128]{2,1,0:T(8,128)(2,1)S(1)}, bf16[16,128,128]{2,1,0:T(8,128)(2,1)S(1)}, u32[]{:S(2)}, u32[]{:S(2)}) collective-permute-start(bf16[16,128,128]{2,1,0:T(8,128)(2,1)S(1)} %get-tuple-element.97), channel_id=1, source_target_pairs={{1,8},{3,10},{5,12},{7,14},{8,1},{9,16},{10,3},{11,18},{12,5},{13,... | collective-permute-start | bytes 1572872 | tf_op jit(solution)/shard_map/ppermute | solution.py:328
  56.6 15.7 %collective-permute-start.16 = (bf16[16,128,128]{2,1,0:T(8,128)(2,1)S(1)}, bf16[16,128,128]{2,1,0:T(8,128)(2,1)S(1)}, u32[]{:S(2)}, u32[]{:S(2)}) collective-permute-start(bf16[16,128,128]{2,1,0:T(8,128)(2,1)S(1)} %get-tuple-element.108), channel_id=1, source_target_pairs={{0,2},{1,0},{2,6},{3,4},{4,3},{5,1},{6,7},{7,5},{8,10},{9,8},{10,1... | collective-permute-start | bytes 1572872 | tf_op jit(solution)/shard_map/ppermute | solution.py:328
  56.7 15.6 %collective-permute-start.17 = (bf16[16,128,128]{2,1,0:T(8,128)(2,1)S(1)}, bf16[16,128,128]{2,1,0:T(8,128)(2,1)S(1)}, u32[]{:S(2)}, u32[]{:S(2)}) collective-permute-start(bf16[16,128,128]{2,1,0:T(8,128)(2,1)S(1)} %get-tuple-element.109), channel_id=1, source_target_pairs={{0,4},{1,6},{2,0},{3,2},{4,5},{5,7},{6,1},{7,3},{8,12},{9,14},{10,... | collective-permute-start | bytes 1572872 | tf_op jit(solution)/shard_map/ppermute | solution.py:328
  73.1 10.7 %collective-permute-start.19 = (bf16[16,128,128]{2,1,0:T(8,128)(2,1)S(1)}, bf16[16,128,128]{2,1,0:T(8,128)(2,1)S(1)}, u32[]{:S(2)}, u32[]{:S(2)}) collective-permute-start(bf16[16,128,128]{2,1,0:T(8,128)(2,1)S(1)} %get-tuple-element.121), channel_id=1, source_target_pairs={{0,1},{1,0},{2,3},{3,2},{4,5},{5,4},{6,7},{7,6},{8,9},{9,8},{10,11... | collective-permute-start | bytes 1572872 | tf_op jit(solution)/shard_map/ppermute | solution.py:328
  73.2 13.6 %collective-permute-start.18 = (bf16[16,128,128]{2,1,0:T(8,128)(2,1)S(1)}, bf16[16,128,128]{2,1,0:T(8,128)(2,1)S(1)}, u32[]{:S(2)}, u32[]{:S(2)}) collective-permute-start(bf16[16,128,128]{2,1,0:T(8,128)(2,1)S(1)} %get-tuple-element.120), channel_id=1, source_target_pairs={{1,8},{3,10},{5,12},{7,14},{8,1},{9,16},{10,3},{11,18},{12,5},{13,... | collective-permute-start | bytes 1572872 | tf_op jit(solution)/shard_map/ppermute | solution.py:328
  89.9 10.5 %collective-permute-start.20 = (f32[2,2,128,128]{3,2,1,0:T(8,128)S(1)}, f32[2,2,128,128]{3,2,1,0:T(8,128)S(1)}, u32[]{:S(2)}, u32[]{:S(2)}) collective-permute-start(f32[2,2,128,128]{3,2,1,0:T(8,128)S(1)} %get-tuple-element.129), channel_id=1, source_target_pairs={{1,4},{3,6},{4,1},{6,3},{9,12},{11,14},{12,9},{14,11},{17,20},{19,... | collective-permute-start | bytes 786440 | tf_op jit(solution)/shard_map/ppermute | solution.py:328
  91.8 8.6 %collective-permute-start.21 = (f32[2,2,128,128]{3,2,1,0:T(8,128)S(1)}, f32[2,2,128,128]{3,2,1,0:T(8,128)S(1)}, u32[]{:S(2)}, u32[]{:S(2)}) collective-permute-start(f32[2,2,128,128]{3,2,1,0:T(8,128)S(1)} %get-tuple-element.130), channel_id=1, source_target_pairs={{0,2},{1,6},{2,0},{3,4},{4,3},{5,7},{6,1},{7,5},{8,10},{9,14},{10,... | collective-permute-start | bytes 786440 | tf_op jit(solution)/shard_map/ppermute | solution.py:328
  100.5 1.4 %collective-permute-start.22 = (f32[2,128,128]{2,1,0:T(8,128)S(1)}, f32[2,128,128]{2,1,0:T(8,128)S(1)}, u32[]{:S(2)}, u32[]{:S(2)}) collective-permute-start(f32[2,128,128]{2,1,0:T(8,128)S(1)} %select_bitcast_fusion), channel_id=1, source_target_pairs={{0,1},{1,0},{2,3},{3,2},{4,5},{5,4},{6,7},{7,6},{8,9},{9,8},{10,11... | collective-permute-start | bytes 393224 | tf_op jit(solution)/shard_map/ppermute | solution.py:328

commit v2 on v1

--- a/solution.py
+++ b/solution.py
@@ -9,10 +9,10 @@
 
 GROUP = 8
 QUADS = 4
-PIECES = 2
+SHARE = 0.625
 ORDER = (0, 3, 1, 2)
 ROWS = 16
-DEPTH = 16
+DEPTH = 24
 LIMIT = 32 * 1024 * 1024
 SMALL = 6 * 1024 * 1024
 VMEM = pl.BlockSpec(memory_space=pltpu.VMEM)
@@ -205,7 +205,7 @@
 
 def products(tiles, weights, acc, nz):
     count, w = tiles[0][0].shape[-3:-1]
-    depth = next(d for d in (DEPTH, 8, 4, 2, 1) if count % d == 0)
+    depth = next(d for d in range(min(DEPTH, count), 0, -1) if count % d == 0)
     pair = 2 if depth % 2 == 0 else 1
 
     def part(step):
@@ -315,8 +315,9 @@
     quad, core = local >> 1, local & 1
     where = jnp.stack([layer, local, quad, core, here, tiles]).astype(jnp.int32)
     count = factors.shape[1] // QUADS
-    pieces = PIECES if count % PIECES == 0 else 1
-    size = count // pieces
+    sizes = [int(count * SHARE)]
+    sizes = [sizes[0], count - sizes[0]] if 0 < sizes[0] < count else [count]
+    pieces = len(sizes)
 
     def send(value, target):
         pairs = []
@@ -328,8 +329,8 @@
         return lax.ppermute(value, "tile", pairs)
 
     def cut(piece, t):
-        start = (t ^ (local & 3)) * count + piece * size
-        return lax.dynamic_slice_in_dim(factors[0], start, size, axis=0)
+        start = (t ^ (local & 3)) * count + sum(sizes[:piece])
+        return lax.dynamic_slice_in_dim(factors[0], start, sizes[piece], axis=0)
 
     def spread(part, t):
         return send(part, lambda z, q, k: (z, t ^ ((q & 1) * 2 + k), q >> 1))
@@ -355,11 +356,13 @@
     for piece in range(1, pieces):
         parts.append({t: spread(own[piece][t], t) for t in ORDER})
     mine = join([load] + turns)
-    mine, parts[0] = lax.optimization_barrier((mine, parts[0]))
+    for t in ORDER[:3]:
+        mine, parts[0][t] = lax.optimization_barrier((mine, parts[0][t]))
     other = to_core(mine)
     half = mix(where, mine, sibling, mine, nz, terms, layers)
-    half, parts[0] = lax.optimization_barrier((half, parts[0]))
     weights = mix(where, mine, other, other, nz, terms, layers, (half,))
+    for t in ORDER[3:]:
+        weights, parts[0][t] = lax.optimization_barrier((weights, parts[0][t]))
 
     def halves(parts, own):
         held, mid, halo = sort(where, [parts[t] for t in range(QUADS)], own)

time: 103 us -> 109 us (1.058); the launches traced: 103 us -> 107 us
  starting transfers between devices: 35.4 us -> 44.4 us
  waiting for transfers between devices: 29.8 us -> 24 us
    ppermute x23, starting transfers between devices: 35.4 us -> 44.4 us  [send(): return lax.ppermute(value, 'tile', pairs)]
    ppermute x23, waiting for transfers between devices: 29.8 us -> 24 us  [send(): return lax.ppermute(value, 'tile', pairs)]
    dynamic_slice x1 -> x2, local copies, waits for them, and re-layouts: 2.7 us -> 3.42 us  [cut(): return lax.dynamic_slice_in_dim(factors[0], start, sizes[piece], axis=0)]
  transfers between devices with their start and end apart: 23 -> 23, of which waited for: 8 -> 9; matrix products, arithmetic and copies ran while one was open for 3% -> 3% of each run, Pallas kernels for 27% -> 27%
where the time goes in v2:
time: 109 us; the launch traced here: 107 us
  starting transfers between devices  44.4 us (41%)
  Pallas kernels  33.9 us (31%)
  waiting for transfers between devices  24 us (22%)
  local copies, waits for them, and re-layouts  3.51 us (3%)
    ppermute x23, starting transfers between devices, send(): return lax.ppermute(value, 'tile', pairs)  44.4 us
    ppermute x23, waiting for transfers between devices, send(): return lax.ppermute(value, 'tile', pairs)  24 us
    pallas_call x6, Pallas kernels, ladder(): pl.pallas_call(kernel, out_shape=shape, in_specs=[SMEM] + [VMEM] * len(ar...  22.5 us
    pallas_call x2, Pallas kernels, mix(): pl.pallas_call(functools.partial(mix_kernel, terms, layers), out_shape=se...  8.07 us
    dynamic_slice x2, local copies, waits for them, and re-layouts, cut(): return lax.dynamic_slice_in_dim(factors[0], start, sizes[piece], axis=0)  3.42 us
  transfers between devices with their start and end apart: 23, of which 9 were waited for; matrix products, arithmetic and copies ran while one was open for 3% of the time, Pallas kernels for 27%

profile of v2, /device:TPU:1, one launch (start us, length us, event | category | flops | bytes accessed | tf_op | source)
XLA Modules:
  0.0 106.9 jit_solution(17693742705228795982)
XLA Ops:
  0.0 1.5 %pack.1.refs_0_ = bf16[1,272,128]{2,1,0:T(8,128)(2,1)} custom-call(bf16[2,128,128]{2,1,0:T(8,128)(2,1)} %refs_0_.1, s32[2,13]{1,0:T(2,128)} %refs_1_.1, s32[2,13]{1,0:T(2,128)} %refs_2_.1, s32[2,13]{1,0:T(2,128)} %refs_3_.1, s32[2,13]{1,0:T(2,128)} %refs_4_.1), custom_call_target="tpu_custom_call" | custom-call | tf_op jit(solution)/shard_map/pack/pallas_call | solution.py:53
  1.5 0.1 stack.23.where
  1.6 2.0 %collective-permute-start = (bf16[1,272,128]{2,1,0:T(8,128)(2,1)}, bf16[1,272,128]{2,1,0:T(8,128)(2,1)S(1)}, u32[]{:S(2)}, u32[]{:S(2)}) collective-permute-start(bf16[1,272,128]{2,1,0:T(8,128)(2,1)} %pack.1.refs_0_), channel_id=1, source_target_pairs={{0,2},{1,3},{2,0},{3,1},{4,6},{5,7},{6,4},{7,5},{8,10},{9,11},{10,... | collective-permute-start | bytes 208904 | tf_op jit(solution)/shard_map/ppermute | solution.py:329
  3.7 1.2 %collective-permute-start.1 = (bf16[1,272,128]{2,1,0:T(8,128)(2,1)}, bf16[1,272,128]{2,1,0:T(8,128)(2,1)S(1)}, u32[]{:S(2)}, u32[]{:S(2)}) collective-permute-start(bf16[1,272,128]{2,1,0:T(8,128)(2,1)} %pack.1.refs_0_), channel_id=1, source_target_pairs={{0,4},{1,5},{2,6},{3,7},{4,0},{5,1},{6,2},{7,3},{8,12},{9,13},{10,... | collective-permute-start | bytes 208904 | tf_op jit(solution)/shard_map/ppermute | solution.py:329
  4.9 0.0 collective-permute-start.2
  4.9 1.9 %dynamic-slice_bitcast_fusion = (bf16[20,128,128]{2,1,0:T(8,128)(2,1)S(1)}, bf16[20,128,128]{2,1,0:T(8,128)(2,1)S(1)}, bf16[20,128,128]{2,1,0:T(8,128)(2,1)S(1)}, bf16[20,128,128]{2,1,0:T(8,128)(2,1)S(1)}) fusion(bf16[1,128,128,128]{3,2,1,0:T(8,128)(2,1)} %param.6, s32[]{:T(128)S(6)} %select_n.55, s32[]{:T(128)S(6)} %select_n.54, s32[]{:T(128)S(6)} %select_n.53, ...), kind=kLoop, calls=%fused_computation | loop fusion | bytes 5242896 | tf_op jit(solution)/shard_map/dynamic_slice | solution.py:333
  6.8 0.0 copy-start
  6.8 1.6 %dynamic-slice_bitcast_fusion.4 = (bf16[12,128,128]{2,1,0:T(8,128)(2,1)S(1)}, bf16[12,128,128]{2,1,0:T(8,128)(2,1)S(1)}, bf16[12,128,128]{2,1,0:T(8,128)(2,1)S(1)}, bf16[12,128,128]{2,1,0:T(8,128)(2,1)S(1)}) fusion(bf16[1,128,128,128]{3,2,1,0:T(8,128)(2,1)} %param.6, s32[]{:T(128)S(6)} %select_n.59, s32[]{:T(128)S(6)} %select_n.57, s32[]{:T(128)S(6)} %select_n.56, ...), kind=kLoop, calls=%fused_computation.4 | loop fusion | bytes 3145744 | tf_op jit(solution)/shard_map/dynamic_slice | solution.py:333
  8.4 0.0 collective-permute-done.refs_1_
  8.4 0.0 collective-permute-done.1.refs_2_
  8.4 0.8 collective-permute-done.2.refs_3_
  9.2 0.0 copy-done
  9.2 1.3 %collective-permute-start.3 = (bf16[4,272,128]{2,1,0:T(8,128)(2,1)S(1)}, bf16[4,272,128]{2,1,0:T(8,128)(2,1)S(1)}, u32[]{:S(2)}, u32[]{:S(2)}) collective-permute-start(bf16[4,272,128]{2,1,0:T(8,128)(2,1)S(1)} %join.2.refs_0_), channel_id=1, source_target_pairs={{0,8},{1,9},{2,10},{3,11},{4,12},{5,13},{6,14},{7,15},{8,16},{9,17... | collective-permute-start | bytes 835592 | tf_op jit(solution)/shard_map/ppermute | solution.py:329
  10.6 2.6 %collective-permute-start.4 = (bf16[4,272,128]{2,1,0:T(8,128)(2,1)S(1)}, bf16[4,272,128]{2,1,0:T(8,128)(2,1)S(1)}, u32[]{:S(2)}, u32[]{:S(2)}) collective-permute-start(bf16[4,272,128]{2,1,0:T(8,128)(2,1)S(1)} %join.2.refs_0_), channel_id=1, source_target_pairs={{0,1},{1,0},{2,3},{3,2},{4,5},{5,4},{6,7},{7,6},{8,9},{9,8},{10,11... | collective-permute-start | bytes 835592 | tf_op jit(solution)/shard_map/ppermute | solution.py:329
  13.2 2.0 %collective-permute-start.7 = (bf16[20,128,128]{2,1,0:T(8,128)(2,1)S(1)}, bf16[20,128,128]{2,1,0:T(8,128)(2,1)S(1)}, u32[]{:S(2)}, u32[]{:S(2)}) collective-permute-start(bf16[20,128,128]{2,1,0:T(8,128)(2,1)S(1)} %get-tuple-element.91.own_a), channel_id=1, source_target_pairs={{1,2},{2,4},{3,6},{4,1},{5,3},{6,5},{9,10},{10,12},{11,14},{12,9},... | collective-permute-start | bytes 1966088 | tf_op jit(solution)/shard_map/ppermute | solution.py:329
  15.3 3.5 %collective-permute-start.8 = (bf16[20,128,128]{2,1,0:T(8,128)(2,1)S(1)}, bf16[20,128,128]{2,1,0:T(8,128)(2,1)S(1)}, u32[]{:S(2)}, u32[]{:S(2)}) collective-permute-start(bf16[20,128,128]{2,1,0:T(8,128)(2,1)S(1)} %get-tuple-element.92.own_d), channel_id=1, source_target_pairs={{0,6},{1,4},{3,0},{4,7},{6,3},{7,1},{8,14},{9,12},{11,8},{12,15},{... | collective-permute-start | bytes 1966088 | tf_op jit(solution)/shard_map/ppermute | solution.py:329
  18.8 0.0 collective-permute-done.3.refs_1_
  18.8 0.0 collective-permute-done.4.lists_other
  18.8 1.4 %collective-permute-start.9 = (bf16[20,128,128]{2,1,0:T(8,128)(2,1)S(1)}, bf16[20,128,128]{2,1,0:T(8,128)(2,1)S(1)}, u32[]{:S(2)}, u32[]{:S(2)}) collective-permute-start(bf16[20,128,128]{2,1,0:T(8,128)(2,1)S(1)} %get-tuple-element.84), channel_id=1, source_target_pairs={{0,2},{1,0},{2,6},{3,4},{4,3},{5,1},{6,7},{7,5},{8,10},{9,8},{10,1... | collective-permute-start | bytes 1966088 | tf_op jit(solution)/shard_map/ppermute | solution.py:329
  20.2 1.3 %collective-permute-start.5 = (bf16[4,272,128]{2,1,0:T(8,128)(2,1)S(1)}, bf16[4,272,128]{2,1,0:T(8,128)(2,1)S(1)}, u32[]{:S(2)}, u32[]{:S(2)}) collective-permute-start(bf16[4,272,128]{2,1,0:T(8,128)(2,1)S(1)} %join.2.refs_0_), channel_id=1, source_target_pairs={{0,16},{1,17},{2,18},{3,19},{4,20},{5,21},{6,22},{7,23},{8,24},{9,... | collective-permute-start | bytes 835592 | tf_op jit(solution)/shard_map/ppermute | solution.py:329
  21.5 1.1 collective-permute-start.6
  22.6 13.1 %collective-permute-done.5.refs_2_ = bf16[4,272,128]{2,1,0:T(8,128)(2,1)S(1)} collective-permute-done((bf16[4,272,128]{2,1,0:T(8,128)(2,1)S(1)}, bf16[4,272,128]{2,1,0:T(8,128)(2,1)S(1)}, u32[]{:S(2)}, u32[]{:S(2)}) %collective-permute-start.5) | collective-permute-done | bytes 278560 | tf_op jit(solution)/shard_map/ppermute | solution.py:329
  35.7 0.0 collective-permute-done.6.refs_3_
  35.7 0.1 join.3.lists_mine.amps
  35.8 0.5 collective-permute-done.7.a
  36.3 2.6 %collective-permute-done.8.d = bf16[20,128,128]{2,1,0:T(8,128)(2,1)S(1)} collective-permute-done((bf16[20,128,128]{2,1,0:T(8,128)(2,1)S(1)}, bf16[20,128,128]{2,1,0:T(8,128)(2,1)S(1)}, u32[]{:S(2)}, u32[]{:S(2)}) %collective-permute-start.8) | collective-permute-done | bytes 655392 | tf_op jit(solution)/shard_map/ppermute | solution.py:329
  38.8 0.3 collective-permute-done.9.b
  39.2 0.0 collective-permute-start.10
  39.2 0.6 collective-permute-start.11
  39.8 3.4 %collective-permute-start.13 = (bf16[12,128,128]{2,1,0:T(8,128)(2,1)S(1)}, bf16[12,128,128]{2,1,0:T(8,128)(2,1)S(1)}, u32[]{:S(2)}, u32[]{:S(2)}) collective-permute-start(bf16[12,128,128]{2,1,0:T(8,128)(2,1)S(1)} %get-tuple-element.95.own_a), channel_id=1, source_target_pairs={{1,2},{2,4},{3,6},{4,1},{5,3},{6,5},{9,10},{10,12},{11,14},{12,9},... | collective-permute-start | bytes 1179656 | tf_op jit(solution)/shard_map/ppermute | solution.py:329
  43.2 3.9 %mix.2.refs_0_ = f32[4,18,128,128]{3,2,1,0:T(8,128)S(1)} custom-call(s32[6]{0:T(128)S(1)} %stack.23.where, bf16[16,272,128]{2,1,0:T(8,128)(2,1)S(1)} %join.3.lists_mine.amps, bf16[4,272,128]{2,1,0:T(8,128)(2,1)S(1)} %collective-permute-done.4.lists_other, bf16[16,272,128]{2,1,0:T(8,128)(2,1)S(1)} %join.3.lists_mine.amps), custom_call_target="tpu_custom_call" | custom-call | tf_op jit(solution)/shard_map/mix/pallas_call | solution.py:126
  47.1 0.0 collective-permute-done.10.lists_other.amps
  47.1 4.2 %mix.3.weights = bf16[4,768,384]{2,1,0:T(8,128)(2,1)S(1)} custom-call(s32[6]{0:T(128)S(1)} %stack.23.where, bf16[16,272,128]{2,1,0:T(8,128)(2,1)S(1)} %join.3.lists_mine.amps, bf16[16,272,128]{2,1,0:T(8,128)(2,1)S(1)} %collective-permute-done.10.lists_other.amps, bf16[16,272,128]{2,1,0:T(8,128)(2,1)S(1)} %collective-permute-done.10.lists_other.amps, ...), custom_call_target="tpu_custom_call" | custom-call | tf_op jit(solution)/shard_map/mix/pallas_call | solution.py:126
  51.3 0.0 collective-permute-done.11.c
  51.3 0.9 sort.2
  52.2 2.8 %collective-permute-start.14 = (bf16[20,128,128]{2,1,0:T(8,128)(2,1)S(1)}, bf16[20,128,128]{2,1,0:T(8,128)(2,1)S(1)}, u32[]{:S(2)}, u32[]{:S(2)}) collective-permute-start(bf16[20,128,128]{2,1,0:T(8,128)(2,1)S(1)} %get-tuple-element.97), channel_id=1, source_target_pairs={{0,1},{1,0},{2,3},{3,2},{4,5},{5,4},{6,7},{7,6},{8,9},{9,8},{10,11... | collective-permute-start | bytes 1966088 | tf_op jit(solution)/shard_map/ppermute | solution.py:329
  55.0 2.6 %collective-permute-start.12 = (bf16[20,128,128]{2,1,0:T(8,128)(2,1)S(1)}, bf16[20,128,128]{2,1,0:T(8,128)(2,1)S(1)}, u32[]{:S(2)}, u32[]{:S(2)}) collective-permute-start(bf16[20,128,128]{2,1,0:T(8,128)(2,1)S(1)} %get-tuple-element.93), channel_id=1, source_target_pairs={{1,8},{3,10},{5,12},{7,14},{8,1},{9,16},{10,3},{11,18},{12,5},{13,... | collective-permute-start | bytes 1966088 | tf_op jit(solution)/shard_map/ppermute | solution.py:329
  57.6 2.1 %collective-permute-start.15 = (bf16[12,128,128]{2,1,0:T(8,128)(2,1)S(1)}, bf16[12,128,128]{2,1,0:T(8,128)(2,1)S(1)}, u32[]{:S(2)}, u32[]{:S(2)}) collective-permute-start(bf16[12,128,128]{2,1,0:T(8,128)(2,1)S(1)} %get-tuple-element.100.own_d), channel_id=1, source_target_pairs={{0,6},{1,4},{3,0},{4,7},{6,3},{7,1},{8,14},{9,12},{11,8},{12,15},{... | collective-permute-start | bytes 1179656 | tf_op jit(solution)/shard_map/ppermute | solution.py:329
  59.7 0.1 collective-permute-start.16
  59.8 0.0 collective-permute-done.13.a
  59.8 4.3 %collective-permute-start.17 = (bf16[12,128,128]{2,1,0:T(8,128)(2,1)S(1)}, bf16[12,128,128]{2,1,0:T(8,128)(2,1)S(1)}, u32[]{:S(2)}, u32[]{:S(2)}) collective-permute-start(bf16[12,128,128]{2,1,0:T(8,128)(2,1)S(1)} %get-tuple-element.105), channel_id=1, source_target_pairs={{0,4},{1,6},{2,0},{3,2},{4,5},{5,7},{6,1},{7,3},{8,12},{9,14},{10,... | collective-permute-start | bytes 1179656 | tf_op jit(solution)/shard_map/ppermute | solution.py:329
  64.1 6.2 %inner.2.refs_0_ = f32[2,2,128,128]{3,2,1,0:T(8,128)S(1)} custom-call(s32[6]{0:T(128)S(1)} %stack.23.where, bf16[4,20,128,128]{3,2,1,0:T(8,128)(2,1)S(1)} %get-tuple-element.96.held, bf16[4,768,384]{2,1,0:T(8,128)(2,1)S(1)} %mix.3.weights), custom_call_target="tpu_custom_call" | custom-call | tf_op jit(solution)/shard_map/inner/pallas_call | solution.py:296
  70.4 0.0 collective-permute-done.14.outside
  70.4 0.0 collective-permute-done.15.d
  70.4 3.6 %beside.2.refs_0_ = f32[2,128,128]{2,1,0:T(8,128)S(1)} custom-call(s32[6]{0:T(128)S(1)} %stack.23.where, bf16[4,20,128,128]{3,2,1,0:T(8,128)(2,1)S(1)} %get-tuple-element.96.held, bf16[20,128,128]{2,1,0:T(8,128)(2,1)S(1)} %collective-permute-done.14.outside, bf16[4,768,384]{2,1,0:T(8,128)(2,1)S(1)} %mix.3.weights), custom_call_target="tpu_custom_call" | custom-call | tf_op jit(solution)/shard_map/beside/pallas_call | solution.py:296
  73.9 0.0 collective-permute-done.12.outside
  74.0 0.9 collective-permute-done.16.b
  74.8 0.0 collective-permute-done.17.c
  74.8 0.8 sort.3
  75.6 0.1 collective-permute-start.19
  75.7 4.9 %collective-permute-start.18 = (bf16[12,128,128]{2,1,0:T(8,128)(2,1)S(1)}, bf16[12,128,128]{2,1,0:T(8,128)(2,1)S(1)}, u32[]{:S(2)}, u32[]{:S(2)}) collective-permute-start(bf16[12,128,128]{2,1,0:T(8,128)(2,1)S(1)} %get-tuple-element.116), channel_id=1, source_target_pairs={{1,8},{3,10},{5,12},{7,14},{8,1},{9,16},{10,3},{11,18},{12,5},{13,... | collective-permute-start | bytes 1179656 | tf_op jit(solution)/shard_map/ppermute | solution.py:329
  80.7 3.6 %beyond.2.refs_0_ = f32[2,128,128]{2,1,0:T(8,128)S(1)} custom-call(s32[6]{0:T(128)S(1)} %stack.23.where, bf16[4,20,128,128]{3,2,1,0:T(8,128)(2,1)S(1)} %get-tuple-element.96.held, bf16[20,128,128]{2,1,0:T(8,128)(2,1)S(1)} %collective-permute-done.12.outside, bf16[4,768,384]{2,1,0:T(8,128)(2,1)S(1)} %mix.3.weights), custom_call_target="tpu_custom_call" | custom-call | tf_op jit(solution)/shard_map/beyond/pallas_call | solution.py:296
  84.2 4.1 %inner.3.refs_1_ = f32[2,2,128,128]{3,2,1,0:T(8,128)S(1)} custom-call(s32[6]{0:T(128)S(1)} %stack.23.where, bf16[4,12,128,128]{3,2,1,0:T(8,128)(2,1)S(1)} %get-tuple-element.115.held, bf16[4,768,384]{2,1,0:T(8,128)(2,1)S(1)} %mix.3.weights, f32[2,2,128,128]{3,2,1,0:T(8,128)S(1)} %inner.2.refs_0_), custom_call_target="tpu_custom_call" | custom-call | tf_op jit(solution)/shard_map/inner/pallas_call | solution.py:296
  88.3 0.0 collective-permute-done.19.outside
  88.3 2.5 %beside.3.refs_2_ = f32[2,128,128]{2,1,0:T(8,128)S(1)} custom-call(s32[6]{0:T(128)S(1)} %stack.23.where, bf16[4,12,128,128]{3,2,1,0:T(8,128)(2,1)S(1)} %get-tuple-element.115.held, bf16[12,128,128]{2,1,0:T(8,128)(2,1)S(1)} %collective-permute-done.19.outside, bf16[4,768,384]{2,1,0:T(8,128)(2,1)S(1)} %mix.3.weights, f32[2,128,128]{2,1,0:T(8,128)S(1)} %beside.2.refs_0_), custom_call_target="tpu_custom_call" | custom-call | tf_op jit(solution)/shard_map/beside/pallas_call | solution.py:296
  90.8 0.0 collective-permute-done.18.outside
  90.8 2.6 %beyond.3 = (f32[2,2,128,128]{3,2,1,0:T(8,128)S(1)}, f32[2,2,128,128]{3,2,1,0:T(8,128)S(1)}) custom-call(s32[6]{0:T(128)S(1)} %stack.23.where, bf16[4,12,128,128]{3,2,1,0:T(8,128)(2,1)S(1)} %get-tuple-element.115.held, bf16[12,128,128]{2,1,0:T(8,128)(2,1)S(1)} %collective-permute-done.18.outside, bf16[4,768,384]{2,1,0:T(8,128)(2,1)S(1)} %mix.3.weights, ...), custom_call_target="tpu_custom_call" | custom-call | tf_op jit(solution)/shard_map/beyond/pallas_call | solution.py:296
  93.4 0.1 collective-permute-start.21
  93.5 6.7 %collective-permute-start.20 = (f32[2,2,128,128]{3,2,1,0:T(8,128)S(1)}, f32[2,2,128,128]{3,2,1,0:T(8,128)S(1)}, u32[]{:S(2)}, u32[]{:S(2)}) collective-permute-start(f32[2,2,128,128]{3,2,1,0:T(8,128)S(1)} %get-tuple-element.125), channel_id=1, source_target_pairs={{1,4},{3,6},{4,1},{6,3},{9,12},{11,14},{12,9},{14,11},{17,20},{19,... | collective-permute-start | bytes 786440 | tf_op jit(solution)/shard_map/ppermute | solution.py:329
  100.3 1.7 %collective-permute-done.21 = f32[2,2,128,128]{3,2,1,0:T(8,128)S(1)} collective-permute-done((f32[2,2,128,128]{3,2,1,0:T(8,128)S(1)}, f32[2,2,128,128]{3,2,1,0:T(8,128)S(1)}, u32[]{:S(2)}, u32[]{:S(2)}) %collective-permute-start.21) | collective-permute-done | bytes 262176 | tf_op jit(solution)/shard_map/ppermute | solution.py:329
  102.0 2.8 %collective-permute-done.20 = f32[2,2,128,128]{3,2,1,0:T(8,128)S(1)} collective-permute-done((f32[2,2,128,128]{3,2,1,0:T(8,128)S(1)}, f32[2,2,128,128]{3,2,1,0:T(8,128)S(1)}, u32[]{:S(2)}, u32[]{:S(2)}) %collective-permute-start.20) | collective-permute-done | bytes 262176 | tf_op jit(solution)/shard_map/ppermute | solution.py:329
  104.8 0.1 collective-permute-start.22
  104.9 1.3 %collective-permute-done.22 = f32[2,128,128]{2,1,0:T(8,128)S(1)} collective-permute-done((f32[2,128,128]{2,1,0:T(8,128)S(1)}, f32[2,128,128]{2,1,0:T(8,128)S(1)}, u32[]{:S(2)}, u32[]{:S(2)}) %collective-permute-start.22) | collective-permute-done | bytes 131104 | tf_op jit(solution)/shard_map/ppermute | solution.py:329
  106.2 0.7 fusion
  (3 shorter events, 0.1 us)
Async XLA Ops:
  1.6 6.8 %collective-permute-start = (bf16[1,272,128]{2,1,0:T(8,128)(2,1)}, bf16[1,272,128]{2,1,0:T(8,128)(2,1)S(1)}, u32[]{:S(2)}, u32[]{:S(2)}) collective-permute-start(bf16[1,272,128]{2,1,0:T(8,128)(2,1)} %pack.1.refs_0_), channel_id=1, source_target_pairs={{0,2},{1,3},{2,0},{3,1},{4,6},{5,7},{6,4},{7,5},{8,10},{9,11},{10,... | collective-permute-start | bytes 208904 | tf_op jit(solution)/shard_map/ppermute | solution.py:329
  3.7 4.7 %collective-permute-start.1 = (bf16[1,272,128]{2,1,0:T(8,128)(2,1)}, bf16[1,272,128]{2,1,0:T(8,128)(2,1)S(1)}, u32[]{:S(2)}, u32[]{:S(2)}) collective-permute-start(bf16[1,272,128]{2,1,0:T(8,128)(2,1)} %pack.1.refs_0_), channel_id=1, source_target_pairs={{0,4},{1,5},{2,6},{3,7},{4,0},{5,1},{6,2},{7,3},{8,12},{9,13},{10,... | collective-permute-start | bytes 208904 | tf_op jit(solution)/shard_map/ppermute | solution.py:329
  4.9 4.3 %collective-permute-start.2 = (bf16[1,272,128]{2,1,0:T(8,128)(2,1)}, bf16[1,272,128]{2,1,0:T(8,128)(2,1)S(1)}, u32[]{:S(2)}, u32[]{:S(2)}) collective-permute-start(bf16[1,272,128]{2,1,0:T(8,128)(2,1)} %pack.1.refs_0_), channel_id=1, source_target_pairs={{0,6},{1,7},{2,4},{3,5},{4,2},{5,3},{6,0},{7,1},{8,14},{9,15},{10,... | collective-permute-start | bytes 208904 | tf_op jit(solution)/shard_map/ppermute | solution.py:329
  6.8 2.4 %copy-start = (bf16[1,272,128]{2,1,0:T(8,128)(2,1)S(1)}, bf16[1,272,128]{2,1,0:T(8,128)(2,1)}, u32[]{:S(2)}) copy-start(bf16[1,272,128]{2,1,0:T(8,128)(2,1)} %pack.1.refs_0_) | copy-start | bytes 208900
  9.2 9.6 %collective-permute-start.3 = (bf16[4,272,128]{2,1,0:T(8,128)(2,1)S(1)}, bf16[4,272,128]{2,1,0:T(8,128)(2,1)S(1)}, u32[]{:S(2)}, u32[]{:S(2)}) collective-permute-start(bf16[4,272,128]{2,1,0:T(8,128)(2,1)S(1)} %join.2.refs_0_), channel_id=1, source_target_pairs={{0,8},{1,9},{2,10},{3,11},{4,12},{5,13},{6,14},{7,15},{8,16},{9,17... | collective-permute-start | bytes 835592 | tf_op jit(solution)/shard_map/ppermute | solution.py:329
  10.6 8.2 %collective-permute-start.4 = (bf16[4,272,128]{2,1,0:T(8,128)(2,1)S(1)}, bf16[4,272,128]{2,1,0:T(8,128)(2,1)S(1)}, u32[]{:S(2)}, u32[]{:S(2)}) collective-permute-start(bf16[4,272,128]{2,1,0:T(8,128)(2,1)S(1)} %join.2.refs_0_), channel_id=1, source_target_pairs={{0,1},{1,0},{2,3},{3,2},{4,5},{5,4},{6,7},{7,6},{8,9},{9,8},{10,11... | collective-permute-start | bytes 835592 | tf_op jit(solution)/shard_map/ppermute | solution.py:329
  13.2 23.1 %collective-permute-start.7 = (bf16[20,128,128]{2,1,0:T(8,128)(2,1)S(1)}, bf16[20,128,128]{2,1,0:T(8,128)(2,1)S(1)}, u32[]{:S(2)}, u32[]{:S(2)}) collective-permute-start(bf16[20,128,128]{2,1,0:T(8,128)(2,1)S(1)} %get-tuple-element.91.own_a), channel_id=1, source_target_pairs={{1,2},{2,4},{3,6},{4,1},{5,3},{6,5},{9,10},{10,12},{11,14},{12,9},... | collective-permute-start | bytes 1966088 | tf_op jit(solution)/shard_map/ppermute | solution.py:329
  15.3 23.6 %collective-permute-start.8 = (bf16[20,128,128]{2,1,0:T(8,128)(2,1)S(1)}, bf16[20,128,128]{2,1,0:T(8,128)(2,1)S(1)}, u32[]{:S(2)}, u32[]{:S(2)}) collective-permute-start(bf16[20,128,128]{2,1,0:T(8,128)(2,1)S(1)} %get-tuple-element.92.own_d), channel_id=1, source_target_pairs={{0,6},{1,4},{3,0},{4,7},{6,3},{7,1},{8,14},{9,12},{11,8},{12,15},{... | collective-permute-start | bytes 1966088 | tf_op jit(solution)/shard_map/ppermute | solution.py:329
  18.8 20.3 %collective-permute-start.9 = (bf16[20,128,128]{2,1,0:T(8,128)(2,1)S(1)}, bf16[20,128,128]{2,1,0:T(8,128)(2,1)S(1)}, u32[]{:S(2)}, u32[]{:S(2)}) collective-permute-start(bf16[20,128,128]{2,1,0:T(8,128)(2,1)S(1)} %get-tuple-element.84), channel_id=1, source_target_pairs={{0,2},{1,0},{2,6},{3,4},{4,3},{5,1},{6,7},{7,5},{8,10},{9,8},{10,1... | collective-permute-start | bytes 1966088 | tf_op jit(solution)/shard_map/ppermute | solution.py:329
  20.2 15.5 %collective-permute-start.5 = (bf16[4,272,128]{2,1,0:T(8,128)(2,1)S(1)}, bf16[4,272,128]{2,1,0:T(8,128)(2,1)S(1)}, u32[]{:S(2)}, u32[]{:S(2)}) collective-permute-start(bf16[4,272,128]{2,1,0:T(8,128)(2,1)S(1)} %join.2.refs_0_), channel_id=1, source_target_pairs={{0,16},{1,17},{2,18},{3,19},{4,20},{5,21},{6,22},{7,23},{8,24},{9,... | collective-permute-start | bytes 835592 | tf_op jit(solution)/shard_map/ppermute | solution.py:329
  21.5 14.1 %collective-permute-start.6 = (bf16[4,272,128]{2,1,0:T(8,128)(2,1)S(1)}, bf16[4,272,128]{2,1,0:T(8,128)(2,1)S(1)}, u32[]{:S(2)}, u32[]{:S(2)}) collective-permute-start(bf16[4,272,128]{2,1,0:T(8,128)(2,1)S(1)} %join.2.refs_0_), channel_id=1, source_target_pairs={{0,24},{1,25},{2,26},{3,27},{4,28},{5,29},{6,30},{7,31},{8,0},{9,1... | collective-permute-start | bytes 835592 | tf_op jit(solution)/shard_map/ppermute | solution.py:329
  39.2 7.9 %collective-permute-start.10 = (bf16[16,272,128]{2,1,0:T(8,128)(2,1)S(1)}, bf16[16,272,128]{2,1,0:T(8,128)(2,1)S(1)}, u32[]{:S(2)}, u32[]{:S(2)}) collective-permute-start(bf16[16,272,128]{2,1,0:T(8,128)(2,1)S(1)} %join.3.lists_mine.amps), channel_id=1, source_target_pairs={{0,1},{1,0},{2,3},{3,2},{4,5},{5,4},{6,7},{7,6},{8,9},{9,8},{10,11... | collective-permute-start | bytes 3342344 | tf_op jit(solution)/shard_map/ppermute | solution.py:329
  39.2 12.1 %collective-permute-start.11 = (bf16[20,128,128]{2,1,0:T(8,128)(2,1)S(1)}, bf16[20,128,128]{2,1,0:T(8,128)(2,1)S(1)}, u32[]{:S(2)}, u32[]{:S(2)}) collective-permute-start(bf16[20,128,128]{2,1,0:T(8,128)(2,1)S(1)} %get-tuple-element.88), channel_id=1, source_target_pairs={{0,4},{1,6},{2,0},{3,2},{4,5},{5,7},{6,1},{7,3},{8,12},{9,14},{10,... | collective-permute-start | bytes 1966088 | tf_op jit(solution)/shard_map/ppermute | solution.py:329
  39.8 20.0 %collective-permute-start.13 = (bf16[12,128,128]{2,1,0:T(8,128)(2,1)S(1)}, bf16[12,128,128]{2,1,0:T(8,128)(2,1)S(1)}, u32[]{:S(2)}, u32[]{:S(2)}) collective-permute-start(bf16[12,128,128]{2,1,0:T(8,128)(2,1)S(1)} %get-tuple-element.95.own_a), channel_id=1, source_target_pairs={{1,2},{2,4},{3,6},{4,1},{5,3},{6,5},{9,10},{10,12},{11,14},{12,9},... | collective-permute-start | bytes 1179656 | tf_op jit(solution)/shard_map/ppermute | solution.py:329
  52.2 18.1 %collective-permute-start.14 = (bf16[20,128,128]{2,1,0:T(8,128)(2,1)S(1)}, bf16[20,128,128]{2,1,0:T(8,128)(2,1)S(1)}, u32[]{:S(2)}, u32[]{:S(2)}) collective-permute-start(bf16[20,128,128]{2,1,0:T(8,128)(2,1)S(1)} %get-tuple-element.97), channel_id=1, source_target_pairs={{0,1},{1,0},{2,3},{3,2},{4,5},{5,4},{6,7},{7,6},{8,9},{9,8},{10,11... | collective-permute-start | bytes 1966088 | tf_op jit(solution)/shard_map/ppermute | solution.py:329
  55.0 18.9 %collective-permute-start.12 = (bf16[20,128,128]{2,1,0:T(8,128)(2,1)S(1)}, bf16[20,128,128]{2,1,0:T(8,128)(2,1)S(1)}, u32[]{:S(2)}, u32[]{:S(2)}) collective-permute-start(bf16[20,128,128]{2,1,0:T(8,128)(2,1)S(1)} %get-tuple-element.93), channel_id=1, source_target_pairs={{1,8},{3,10},{5,12},{7,14},{8,1},{9,16},{10,3},{11,18},{12,5},{13,... | collective-permute-start | bytes 1966088 | tf_op jit(solution)/shard_map/ppermute | solution.py:329
  57.6 12.8 %collective-permute-start.15 = (bf16[12,128,128]{2,1,0:T(8,128)(2,1)S(1)}, bf16[12,128,128]{2,1,0:T(8,128)(2,1)S(1)}, u32[]{:S(2)}, u32[]{:S(2)}) collective-permute-start(bf16[12,128,128]{2,1,0:T(8,128)(2,1)S(1)} %get-tuple-element.100.own_d), channel_id=1, source_target_pairs={{0,6},{1,4},{3,0},{4,7},{6,3},{7,1},{8,14},{9,12},{11,8},{12,15},{... | collective-permute-start | bytes 1179656 | tf_op jit(solution)/shard_map/ppermute | solution.py:329
  59.7 15.1 %collective-permute-start.16 = (bf16[12,128,128]{2,1,0:T(8,128)(2,1)S(1)}, bf16[12,128,128]{2,1,0:T(8,128)(2,1)S(1)}, u32[]{:S(2)}, u32[]{:S(2)}) collective-permute-start(bf16[12,128,128]{2,1,0:T(8,128)(2,1)S(1)} %get-tuple-element.104), channel_id=1, source_target_pairs={{0,2},{1,0},{2,6},{3,4},{4,3},{5,1},{6,7},{7,5},{8,10},{9,8},{10,1... | collective-permute-start | bytes 1179656 | tf_op jit(solution)/shard_map/ppermute | solution.py:329
  59.8 15.0 %collective-permute-start.17 = (bf16[12,128,128]{2,1,0:T(8,128)(2,1)S(1)}, bf16[12,128,128]{2,1,0:T(8,128)(2,1)S(1)}, u32[]{:S(2)}, u32[]{:S(2)}) collective-permute-start(bf16[12,128,128]{2,1,0:T(8,128)(2,1)S(1)} %get-tuple-element.105), channel_id=1, source_target_pairs={{0,4},{1,6},{2,0},{3,2},{4,5},{5,7},{6,1},{7,3},{8,12},{9,14},{10,... | collective-permute-start | bytes 1179656 | tf_op jit(solution)/shard_map/ppermute | solution.py:329
  75.6 12.7 %collective-permute-start.19 = (bf16[12,128,128]{2,1,0:T(8,128)(2,1)S(1)}, bf16[12,128,128]{2,1,0:T(8,128)(2,1)S(1)}, u32[]{:S(2)}, u32[]{:S(2)}) collective-permute-start(bf16[12,128,128]{2,1,0:T(8,128)(2,1)S(1)} %get-tuple-element.117), channel_id=1, source_target_pairs={{0,1},{1,0},{2,3},{3,2},{4,5},{5,4},{6,7},{7,6},{8,9},{9,8},{10,11... | collective-permute-start | bytes 1179656 | tf_op jit(solution)/shard_map/ppermute | solution.py:329
  75.7 15.1 %collective-permute-start.18 = (bf16[12,128,128]{2,1,0:T(8,128)(2,1)S(1)}, bf16[12,128,128]{2,1,0:T(8,128)(2,1)S(1)}, u32[]{:S(2)}, u32[]{:S(2)}) collective-permute-start(bf16[12,128,128]{2,1,0:T(8,128)(2,1)S(1)} %get-tuple-element.116), channel_id=1, source_target_pairs={{1,8},{3,10},{5,12},{7,14},{8,1},{9,16},{10,3},{11,18},{12,5},{13,... | collective-permute-start | bytes 1179656 | tf_op jit(solution)/shard_map/ppermute | solution.py:329
  93.4 8.6 %collective-permute-start.21 = (f32[2,2,128,128]{3,2,1,0:T(8,128)S(1)}, f32[2,2,128,128]{3,2,1,0:T(8,128)S(1)}, u32[]{:S(2)}, u32[]{:S(2)}) collective-permute-start(f32[2,2,128,128]{3,2,1,0:T(8,128)S(1)} %get-tuple-element.126), channel_id=1, source_target_pairs={{0,2},{1,6},{2,0},{3,4},{4,3},{5,7},{6,1},{7,5},{8,10},{9,14},{10,... | collective-permute-start | bytes 786440 | tf_op jit(solution)/shard_map/ppermute | solution.py:329
  93.5 11.3 %collective-permute-start.20 = (f32[2,2,128,128]{3,2,1,0:T(8,128)S(1)}, f32[2,2,128,128]{3,2,1,0:T(8,128)S(1)}, u32[]{:S(2)}, u32[]{:S(2)}) collective-permute-start(f32[2,2,128,128]{3,2,1,0:T(8,128)S(1)} %get-tuple-element.125), channel_id=1, source_target_pairs={{1,4},{3,6},{4,1},{6,3},{9,12},{11,14},{12,9},{14,11},{17,20},{19,... | collective-permute-start | bytes 786440 | tf_op jit(solution)/shard_map/ppermute | solution.py:329
  104.8 1.4 %collective-permute-start.22 = (f32[2,128,128]{2,1,0:T(8,128)S(1)}, f32[2,128,128]{2,1,0:T(8,128)S(1)}, u32[]{:S(2)}, u32[]{:S(2)}) collective-permute-start(f32[2,128,128]{2,1,0:T(8,128)S(1)} %select_bitcast_fusion), channel_id=1, source_target_pairs={{0,1},{1,0},{2,3},{3,2},{4,5},{5,4},{6,7},{7,6},{8,9},{9,8},{10,11... | collective-permute-start | bytes 393224 | tf_op jit(solution)/shard_map/ppermute | solution.py:329

commit v3 on v2

--- a/solution.py
+++ b/solution.py
@@ -9,10 +9,10 @@
 
 GROUP = 8
 QUADS = 4
-SHARE = 0.625
+SHARE = 0.5
 ORDER = (0, 3, 1, 2)
 ROWS = 16
-DEPTH = 24
+DEPTH = 16
 LIMIT = 32 * 1024 * 1024
 SMALL = 6 * 1024 * 1024
 VMEM = pl.BlockSpec(memory_space=pltpu.VMEM)
@@ -374,27 +374,21 @@
 
     held, mid, halo = halves(parts[0], own[0])
     ahead = list(ORDER) if pieces > 1 else []
-    for t in ahead[:1]:
+    for t in ahead[:2]:
         held, parts[1][t] = lax.optimization_barrier((held, parts[1][t]))
     inner = beside = beyond = None
     for piece in range(pieces):
         last = piece == pieces - 1
         inner = ladder("inner", where, held, [], weights, nz, inner)
         mid, inner = lax.optimization_barrier((mid, inner))
-        for t in ahead[1:2] if piece == 0 else []:
-            mid, parts[1][t] = lax.optimization_barrier((mid, parts[1][t]))
         beside = ladder("beside", where, held, [mid], weights, nz, beside)
         halo, beside = lax.optimization_barrier((halo, beside))
-        now, outside = held, halo
-        if not last:
-            beside, after = lax.optimization_barrier((beside, parts[piece + 1]))
-            held, mid, halo = halves(after, own[piece + 1])
-            held, outside = lax.optimization_barrier((held, outside))
         beyond = ladder(
-            "beyond", where, now, [outside], weights, nz, beyond, (inner, beside) if last else ()
+            "beyond", where, held, [halo], weights, nz, beyond, (inner, beside) if last else ()
         )
         if not last:
-            held, beyond = lax.optimization_barrier((held, beyond))
+            beyond, after = lax.optimization_barrier((beyond, parts[piece + 1]))
+            held, mid, halo = halves(after, own[piece + 1])
 
     stays = (quad >> 1) == core
     pair = jnp.where(stays, beyond[0], 0.0)

time: 109 us -> 103 us (0.945); the launches traced: 107 us -> 103 us
  starting transfers between devices: 44.4 us -> 41.8 us
    ppermute x23, starting transfers between devices: 44.4 us -> 41.8 us  [send(): return lax.ppermute(value, 'tile', pairs)]
    dynamic_slice x2 -> x1, local copies, waits for them, and re-layouts: 3.42 us -> 2.73 us  [cut(): return lax.dynamic_slice_in_dim(factors[0], start, sizes[piece], axis=0)]
  transfers between devices with their start and end apart: 23 -> 23, of which waited for: 9 -> 6; matrix products, arithmetic and copies ran while one was open for 3% -> 3% of each run, Pallas kernels for 27% -> 27%
where the time goes in v3:
time: 103 us
  starting transfers between devices  41.8 us (41%)
  Pallas kernels  33.5 us (33%)
  waiting for transfers between devices  23.6 us (23%)
  local copies, waits for them, and re-layouts  2.82 us (3%)
    ppermute x23, starting transfers between devices, send(): return lax.ppermute(value, 'tile', pairs)  41.8 us
    ppermute x23, waiting for transfers between devices, send(): return lax.ppermute(value, 'tile', pairs)  23.6 us
    pallas_call x6, Pallas kernels, ladder(): pl.pallas_call(kernel, out_shape=shape, in_specs=[SMEM] + [VMEM] * len(ar...  22.1 us
    pallas_call x2, Pallas kernels, mix(): pl.pallas_call(functools.partial(mix_kernel, terms, layers), out_shape=se...  8.07 us
    dynamic_slice x1, local copies, waits for them, and re-layouts, cut(): return lax.dynamic_slice_in_dim(factors[0], start, sizes[piece], axis=0)  2.73 us
  transfers between devices with their start and end apart: 23, of which 6 were waited for; matrix products, arithmetic and copies ran while one was open for 3% of the time, Pallas kernels for 27%

profile of v3, /device:TPU:1, one launch (start us, length us, event | category | flops | bytes accessed | tf_op | source)
XLA Modules:
  0.0 102.8 jit_solution(15509517031528088640)
XLA Ops:
  0.0 1.5 %pack.1.refs_0_ = bf16[1,272,128]{2,1,0:T(8,128)(2,1)} custom-call(bf16[2,128,128]{2,1,0:T(8,128)(2,1)} %refs_0_.1, s32[2,13]{1,0:T(2,128)} %refs_1_.1, s32[2,13]{1,0:T(2,128)} %refs_2_.1, s32[2,13]{1,0:T(2,128)} %refs_3_.1, s32[2,13]{1,0:T(2,128)} %refs_4_.1), custom_call_target="tpu_custom_call" | custom-call | tf_op jit(solution)/shard_map/pack/pallas_call | solution.py:53
  1.5 0.1 stack.23.where
  1.6 2.0 %collective-permute-start = (bf16[1,272,128]{2,1,0:T(8,128)(2,1)}, bf16[1,272,128]{2,1,0:T(8,128)(2,1)S(1)}, u32[]{:S(2)}, u32[]{:S(2)}) collective-permute-start(bf16[1,272,128]{2,1,0:T(8,128)(2,1)} %pack.1.refs_0_), channel_id=1, source_target_pairs={{0,2},{1,3},{2,0},{3,1},{4,6},{5,7},{6,4},{7,5},{8,10},{9,11},{10,... | collective-permute-start | bytes 208904 | tf_op jit(solution)/shard_map/ppermute | solution.py:329
  3.7 1.2 %collective-permute-start.1 = (bf16[1,272,128]{2,1,0:T(8,128)(2,1)}, bf16[1,272,128]{2,1,0:T(8,128)(2,1)S(1)}, u32[]{:S(2)}, u32[]{:S(2)}) collective-permute-start(bf16[1,272,128]{2,1,0:T(8,128)(2,1)} %pack.1.refs_0_), channel_id=1, source_target_pairs={{0,4},{1,5},{2,6},{3,7},{4,0},{5,1},{6,2},{7,3},{8,12},{9,13},{10,... | collective-permute-start | bytes 208904 | tf_op jit(solution)/shard_map/ppermute | solution.py:329
  4.9 0.0 collective-permute-start.2
  4.9 0.0 copy-start
  4.9 2.7 %dynamic-slice_bitcast_fusion = (bf16[16,128,128]{2,1,0:T(8,128)(2,1)S(1)}, bf16[16,128,128]{2,1,0:T(8,128)(2,1)S(1)}, bf16[16,128,128]{2,1,0:T(8,128)(2,1)S(1)}...) fusion(bf16[1,128,128,128]{3,2,1,0:T(8,128)(2,1)} %param.6, ...), kind=kLoop, calls=%fused_computation | loop fusion | bytes 8388640 | tf_op jit(solution)/shard_map/dynamic_slice | solution.py:333
  7.7 0.0 collective-permute-done.refs_1_
  7.7 0.0 collective-permute-done.1.refs_2_
  7.7 1.5 %collective-permute-done.2.refs_3_ = bf16[1,272,128]{2,1,0:T(8,128)(2,1)S(1)} collective-permute-done((bf16[1,272,128]{2,1,0:T(8,128)(2,1)}, bf16[1,272,128]{2,1,0:T(8,128)(2,1)S(1)}, u32[]{:S(2)}, u32[]{:S(2)}) %collective-permute-start.2) | collective-permute-done | bytes 69664 | tf_op jit(solution)/shard_map/ppermute | solution.py:329
  9.2 0.0 copy-done
  9.2 1.3 %collective-permute-start.3 = (bf16[4,272,128]{2,1,0:T(8,128)(2,1)S(1)}, bf16[4,272,128]{2,1,0:T(8,128)(2,1)S(1)}, u32[]{:S(2)}, u32[]{:S(2)}) collective-permute-start(bf16[4,272,128]{2,1,0:T(8,128)(2,1)S(1)} %join.2.refs_0_), channel_id=1, source_target_pairs={{0,8},{1,9},{2,10},{3,11},{4,12},{5,13},{6,14},{7,15},{8,16},{9,17... | collective-permute-start | bytes 835592 | tf_op jit(solution)/shard_map/ppermute | solution.py:329
  10.6 2.6 %collective-permute-start.4 = (bf16[4,272,128]{2,1,0:T(8,128)(2,1)S(1)}, bf16[4,272,128]{2,1,0:T(8,128)(2,1)S(1)}, u32[]{:S(2)}, u32[]{:S(2)}) collective-permute-start(bf16[4,272,128]{2,1,0:T(8,128)(2,1)S(1)} %join.2.refs_0_), channel_id=1, source_target_pairs={{0,1},{1,0},{2,3},{3,2},{4,5},{5,4},{6,7},{7,6},{8,9},{9,8},{10,11... | collective-permute-start | bytes 835592 | tf_op jit(solution)/shard_map/ppermute | solution.py:329
  13.2 2.0 %collective-permute-start.7 = (bf16[16,128,128]{2,1,0:T(8,128)(2,1)S(1)}, bf16[16,128,128]{2,1,0:T(8,128)(2,1)S(1)}, u32[]{:S(2)}, u32[]{:S(2)}) collective-permute-start(bf16[16,128,128]{2,1,0:T(8,128)(2,1)S(1)} %get-tuple-element.87.own_a), channel_id=1, source_target_pairs={{1,2},{2,4},{3,6},{4,1},{5,3},{6,5},{9,10},{10,12},{11,14},{12,9},... | collective-permute-start | bytes 1572872 | tf_op jit(solution)/shard_map/ppermute | solution.py:329
  15.3 3.5 %collective-permute-start.8 = (bf16[16,128,128]{2,1,0:T(8,128)(2,1)S(1)}, bf16[16,128,128]{2,1,0:T(8,128)(2,1)S(1)}, u32[]{:S(2)}, u32[]{:S(2)}) collective-permute-start(bf16[16,128,128]{2,1,0:T(8,128)(2,1)S(1)} %get-tuple-element.88.own_d), channel_id=1, source_target_pairs={{0,6},{1,4},{3,0},{4,7},{6,3},{7,1},{8,14},{9,12},{11,8},{12,15},{... | collective-permute-start | bytes 1572872 | tf_op jit(solution)/shard_map/ppermute | solution.py:329
  18.8 0.0 collective-permute-done.3.refs_1_
  18.8 0.0 collective-permute-done.4.lists_other
  18.8 1.4 %collective-permute-start.9 = (bf16[16,128,128]{2,1,0:T(8,128)(2,1)S(1)}, bf16[16,128,128]{2,1,0:T(8,128)(2,1)S(1)}, u32[]{:S(2)}, u32[]{:S(2)}) collective-permute-start(bf16[16,128,128]{2,1,0:T(8,128)(2,1)S(1)} %get-tuple-element.80), channel_id=1, source_target_pairs={{0,2},{1,0},{2,6},{3,4},{4,3},{5,1},{6,7},{7,5},{8,10},{9,8},{10,1... | collective-permute-start | bytes 1572872 | tf_op jit(solution)/shard_map/ppermute | solution.py:329
  20.2 1.3 %collective-permute-start.5 = (bf16[4,272,128]{2,1,0:T(8,128)(2,1)S(1)}, bf16[4,272,128]{2,1,0:T(8,128)(2,1)S(1)}, u32[]{:S(2)}, u32[]{:S(2)}) collective-permute-start(bf16[4,272,128]{2,1,0:T(8,128)(2,1)S(1)} %join.2.refs_0_), channel_id=1, source_target_pairs={{0,16},{1,17},{2,18},{3,19},{4,20},{5,21},{6,22},{7,23},{8,24},{9,... | collective-permute-start | bytes 835592 | tf_op jit(solution)/shard_map/ppermute | solution.py:329
  21.5 1.1 %collective-permute-start.6 = (bf16[4,272,128]{2,1,0:T(8,128)(2,1)S(1)}, bf16[4,272,128]{2,1,0:T(8,128)(2,1)S(1)}, u32[]{:S(2)}, u32[]{:S(2)}) collective-permute-start(bf16[4,272,128]{2,1,0:T(8,128)(2,1)S(1)} %join.2.refs_0_), channel_id=1, source_target_pairs={{0,24},{1,25},{2,26},{3,27},{4,28},{5,29},{6,30},{7,31},{8,0},{9,1... | collective-permute-start | bytes 835592 | tf_op jit(solution)/shard_map/ppermute | solution.py:329
  22.6 13.1 %collective-permute-done.5.refs_2_ = bf16[4,272,128]{2,1,0:T(8,128)(2,1)S(1)} collective-permute-done((bf16[4,272,128]{2,1,0:T(8,128)(2,1)S(1)}, bf16[4,272,128]{2,1,0:T(8,128)(2,1)S(1)}, u32[]{:S(2)}, u32[]{:S(2)}) %collective-permute-start.5) | collective-permute-done | bytes 278560 | tf_op jit(solution)/shard_map/ppermute | solution.py:329
  35.7 0.0 collective-permute-done.6.refs_3_
  35.7 0.1 join.3.lists_mine.amps
  35.8 0.0 collective-permute-done.7.a
  35.8 0.0 collective-permute-done.8.d
  35.8 0.0 collective-permute-done.9.b
  35.8 0.8 collective-permute-start.10
  36.6 0.4 collective-permute-start.11
  37.0 3.2 %collective-permute-start.12 = (bf16[16,128,128]{2,1,0:T(8,128)(2,1)S(1)}, bf16[16,128,128]{2,1,0:T(8,128)(2,1)S(1)}, u32[]{:S(2)}, u32[]{:S(2)}) collective-permute-start(bf16[16,128,128]{2,1,0:T(8,128)(2,1)S(1)} %get-tuple-element.90.own_a), channel_id=1, source_target_pairs={{1,2},{2,4},{3,6},{4,1},{5,3},{6,5},{9,10},{10,12},{11,14},{12,9},... | collective-permute-start | bytes 1572872 | tf_op jit(solution)/shard_map/ppermute | solution.py:329
  40.2 2.3 %collective-permute-start.13 = (bf16[16,128,128]{2,1,0:T(8,128)(2,1)S(1)}, bf16[16,128,128]{2,1,0:T(8,128)(2,1)S(1)}, u32[]{:S(2)}, u32[]{:S(2)}) collective-permute-start(bf16[16,128,128]{2,1,0:T(8,128)(2,1)S(1)} %get-tuple-element.92.own_d), channel_id=1, source_target_pairs={{0,6},{1,4},{3,0},{4,7},{6,3},{7,1},{8,14},{9,12},{11,8},{12,15},{... | collective-permute-start | bytes 1572872 | tf_op jit(solution)/shard_map/ppermute | solution.py:329
  42.6 3.9 %mix.2.refs_0_ = f32[4,18,128,128]{3,2,1,0:T(8,128)S(1)} custom-call(s32[6]{0:T(128)S(1)} %stack.23.where, bf16[16,272,128]{2,1,0:T(8,128)(2,1)S(1)} %join.3.lists_mine.amps, bf16[4,272,128]{2,1,0:T(8,128)(2,1)S(1)} %collective-permute-done.4.lists_other, bf16[16,272,128]{2,1,0:T(8,128)(2,1)S(1)} %join.3.lists_mine.amps), custom_call_target="tpu_custom_call" | custom-call | tf_op jit(solution)/shard_map/mix/pallas_call | solution.py:126
  46.4 0.0 collective-permute-done.10.lists_other.amps
  46.4 4.2 %mix.3.weights = bf16[4,768,384]{2,1,0:T(8,128)(2,1)S(1)} custom-call(s32[6]{0:T(128)S(1)} %stack.23.where, bf16[16,272,128]{2,1,0:T(8,128)(2,1)S(1)} %join.3.lists_mine.amps, bf16[16,272,128]{2,1,0:T(8,128)(2,1)S(1)} %collective-permute-done.10.lists_other.amps, bf16[16,272,128]{2,1,0:T(8,128)(2,1)S(1)} %collective-permute-done.10.lists_other.amps, ...), custom_call_target="tpu_custom_call" | custom-call | tf_op jit(solution)/shard_map/mix/pallas_call | solution.py:126
  50.7 0.0 collective-permute-done.11.c
  50.7 0.8 sort.2
  51.5 1.0 collective-permute-start.15
  52.5 7.8 %collective-permute-start.14 = (bf16[16,128,128]{2,1,0:T(8,128)(2,1)S(1)}, bf16[16,128,128]{2,1,0:T(8,128)(2,1)S(1)}, u32[]{:S(2)}, u32[]{:S(2)}) collective-permute-start(bf16[16,128,128]{2,1,0:T(8,128)(2,1)S(1)} %get-tuple-element.94), channel_id=1, source_target_pairs={{1,8},{3,10},{5,12},{7,14},{8,1},{9,16},{10,3},{11,18},{12,5},{13,... | collective-permute-start | bytes 1572872 | tf_op jit(solution)/shard_map/ppermute | solution.py:329
  60.3 0.1 collective-permute-start.16
  60.4 0.0 collective-permute-done.12.a
  60.4 1.9 %collective-permute-start.17 = (bf16[16,128,128]{2,1,0:T(8,128)(2,1)S(1)}, bf16[16,128,128]{2,1,0:T(8,128)(2,1)S(1)}, u32[]{:S(2)}, u32[]{:S(2)}) collective-permute-start(bf16[16,128,128]{2,1,0:T(8,128)(2,1)S(1)} %get-tuple-element.101), channel_id=1, source_target_pairs={{0,4},{1,6},{2,0},{3,2},{4,5},{5,7},{6,1},{7,3},{8,12},{9,14},{10,... | collective-permute-start | bytes 1572872 | tf_op jit(solution)/shard_map/ppermute | solution.py:329
  62.3 0.0 collective-permute-done.13.d
  62.3 5.0 %inner.2.refs_0_ = f32[2,2,128,128]{3,2,1,0:T(8,128)S(1)} custom-call(s32[6]{0:T(128)S(1)} %stack.23.where, bf16[4,16,128,128]{3,2,1,0:T(8,128)(2,1)S(1)} %get-tuple-element.93.held, bf16[4,768,384]{2,1,0:T(8,128)(2,1)S(1)} %mix.3.weights), custom_call_target="tpu_custom_call" | custom-call | tf_op jit(solution)/shard_map/inner/pallas_call | solution.py:296
  67.3 0.0 collective-permute-done.15.outside
  67.3 3.0 %beside.2.refs_0_ = f32[2,128,128]{2,1,0:T(8,128)S(1)} custom-call(s32[6]{0:T(128)S(1)} %stack.23.where, bf16[4,16,128,128]{3,2,1,0:T(8,128)(2,1)S(1)} %get-tuple-element.93.held, bf16[16,128,128]{2,1,0:T(8,128)(2,1)S(1)} %collective-permute-done.15.outside, bf16[4,768,384]{2,1,0:T(8,128)(2,1)S(1)} %mix.3.weights), custom_call_target="tpu_custom_call" | custom-call | tf_op jit(solution)/shard_map/beside/pallas_call | solution.py:296
  70.3 0.0 collective-permute-done.14.outside
  70.3 3.0 %beyond.2.refs_0_ = f32[2,128,128]{2,1,0:T(8,128)S(1)} custom-call(s32[6]{0:T(128)S(1)} %stack.23.where, bf16[4,16,128,128]{3,2,1,0:T(8,128)(2,1)S(1)} %get-tuple-element.93.held, bf16[16,128,128]{2,1,0:T(8,128)(2,1)S(1)} %collective-permute-done.14.outside, bf16[4,768,384]{2,1,0:T(8,128)(2,1)S(1)} %mix.3.weights), custom_call_target="tpu_custom_call" | custom-call | tf_op jit(solution)/shard_map/beyond/pallas_call | solution.py:296
  73.4 0.0 collective-permute-done.16.b
  73.4 0.7 collective-permute-done.17.c
  74.1 0.8 sort.3
  74.9 0.1 collective-permute-start.19
  75.0 4.4 %collective-permute-start.18 = (bf16[16,128,128]{2,1,0:T(8,128)(2,1)S(1)}, bf16[16,128,128]{2,1,0:T(8,128)(2,1)S(1)}, u32[]{:S(2)}, u32[]{:S(2)}) collective-permute-start(bf16[16,128,128]{2,1,0:T(8,128)(2,1)S(1)} %get-tuple-element.108), channel_id=1, source_target_pairs={{1,8},{3,10},{5,12},{7,14},{8,1},{9,16},{10,3},{11,18},{12,5},{13,... | collective-permute-start | bytes 1572872 | tf_op jit(solution)/shard_map/ppermute | solution.py:329
  79.4 5.0 %inner.3.refs_1_ = f32[2,2,128,128]{3,2,1,0:T(8,128)S(1)} custom-call(s32[6]{0:T(128)S(1)} %stack.23.where, bf16[4,16,128,128]{3,2,1,0:T(8,128)(2,1)S(1)} %get-tuple-element.107.held, bf16[4,768,384]{2,1,0:T(8,128)(2,1)S(1)} %mix.3.weights, f32[2,2,128,128]{3,2,1,0:T(8,128)S(1)} %inner.2.refs_0_), custom_call_target="tpu_custom_call" | custom-call | tf_op jit(solution)/shard_map/inner/pallas_call | solution.py:296
  84.4 0.0 collective-permute-done.19.outside
  84.5 3.0 %beside.3.refs_2_ = f32[2,128,128]{2,1,0:T(8,128)S(1)} custom-call(s32[6]{0:T(128)S(1)} %stack.23.where, bf16[4,16,128,128]{3,2,1,0:T(8,128)(2,1)S(1)} %get-tuple-element.107.held, bf16[16,128,128]{2,1,0:T(8,128)(2,1)S(1)} %collective-permute-done.19.outside, bf16[4,768,384]{2,1,0:T(8,128)(2,1)S(1)} %mix.3.weights, f32[2,128,128]{2,1,0:T(8,128)S(1)} %beside.2.refs_0_), custom_call_target="tpu_custom_call" | custom-call | tf_op jit(solution)/shard_map/beside/pallas_call | solution.py:296
  87.5 0.0 collective-permute-done.18.outside
  87.5 3.1 %beyond.3 = (f32[2,2,128,128]{3,2,1,0:T(8,128)S(1)}, f32[2,2,128,128]{3,2,1,0:T(8,128)S(1)}) custom-call(s32[6]{0:T(128)S(1)} %stack.23.where, bf16[4,16,128,128]{3,2,1,0:T(8,128)(2,1)S(1)} %get-tuple-element.107.held, bf16[16,128,128]{2,1,0:T(8,128)(2,1)S(1)} %collective-permute-done.18.outside, bf16[4,768,384]{2,1,0:T(8,128)(2,1)S(1)} %mix.3.weights, ...), custom_call_target="tpu_custom_call" | custom-call | tf_op jit(solution)/shard_map/beyond/pallas_call | solution.py:296
  90.6 0.1 collective-permute-start.21
  90.7 3.1 %collective-permute-start.20 = (f32[2,2,128,128]{3,2,1,0:T(8,128)S(1)}, f32[2,2,128,128]{3,2,1,0:T(8,128)S(1)}, u32[]{:S(2)}, u32[]{:S(2)}) collective-permute-start(f32[2,2,128,128]{3,2,1,0:T(8,128)S(1)} %get-tuple-element.117), channel_id=1, source_target_pairs={{1,4},{3,6},{4,1},{6,3},{9,12},{11,14},{12,9},{14,11},{17,20},{19,... | collective-permute-start | bytes 786440 | tf_op jit(solution)/shard_map/ppermute | solution.py:329
  93.8 5.0 %collective-permute-done.21 = f32[2,2,128,128]{3,2,1,0:T(8,128)S(1)} collective-permute-done((f32[2,2,128,128]{3,2,1,0:T(8,128)S(1)}, f32[2,2,128,128]{3,2,1,0:T(8,128)S(1)}, u32[]{:S(2)}, u32[]{:S(2)}) %collective-permute-start.21) | collective-permute-done | bytes 262176 | tf_op jit(solution)/shard_map/ppermute | solution.py:329
  98.8 1.9 %collective-permute-done.20 = f32[2,2,128,128]{3,2,1,0:T(8,128)S(1)} collective-permute-done((f32[2,2,128,128]{3,2,1,0:T(8,128)S(1)}, f32[2,2,128,128]{3,2,1,0:T(8,128)S(1)}, u32[]{:S(2)}, u32[]{:S(2)}) %collective-permute-start.20) | collective-permute-done | bytes 262176 | tf_op jit(solution)/shard_map/ppermute | solution.py:329
  100.8 0.1 collective-permute-start.22
  100.8 1.3 %collective-permute-done.22 = f32[2,128,128]{2,1,0:T(8,128)S(1)} collective-permute-done((f32[2,128,128]{2,1,0:T(8,128)S(1)}, f32[2,128,128]{2,1,0:T(8,128)S(1)}, u32[]{:S(2)}, u32[]{:S(2)}) %collective-permute-start.22) | collective-permute-done | bytes 131104 | tf_op jit(solution)/shard_map/ppermute | solution.py:329
  102.2 0.7 fusion
  (3 shorter events, 0.1 us)
Async XLA Ops:
  1.6 6.0 %collective-permute-start = (bf16[1,272,128]{2,1,0:T(8,128)(2,1)}, bf16[1,272,128]{2,1,0:T(8,128)(2,1)S(1)}, u32[]{:S(2)}, u32[]{:S(2)}) collective-permute-start(bf16[1,272,128]{2,1,0:T(8,128)(2,1)} %pack.1.refs_0_), channel_id=1, source_target_pairs={{0,2},{1,3},{2,0},{3,1},{4,6},{5,7},{6,4},{7,5},{8,10},{9,11},{10,... | collective-permute-start | bytes 208904 | tf_op jit(solution)/shard_map/ppermute | solution.py:329
  3.7 4.0 %collective-permute-start.1 = (bf16[1,272,128]{2,1,0:T(8,128)(2,1)}, bf16[1,272,128]{2,1,0:T(8,128)(2,1)S(1)}, u32[]{:S(2)}, u32[]{:S(2)}) collective-permute-start(bf16[1,272,128]{2,1,0:T(8,128)(2,1)} %pack.1.refs_0_), channel_id=1, source_target_pairs={{0,4},{1,5},{2,6},{3,7},{4,0},{5,1},{6,2},{7,3},{8,12},{9,13},{10,... | collective-permute-start | bytes 208904 | tf_op jit(solution)/shard_map/ppermute | solution.py:329
  4.9 4.3 %collective-permute-start.2 = (bf16[1,272,128]{2,1,0:T(8,128)(2,1)}, bf16[1,272,128]{2,1,0:T(8,128)(2,1)S(1)}, u32[]{:S(2)}, u32[]{:S(2)}) collective-permute-start(bf16[1,272,128]{2,1,0:T(8,128)(2,1)} %pack.1.refs_0_), channel_id=1, source_target_pairs={{0,6},{1,7},{2,4},{3,5},{4,2},{5,3},{6,0},{7,1},{8,14},{9,15},{10,... | collective-permute-start | bytes 208904 | tf_op jit(solution)/shard_map/ppermute | solution.py:329
  4.9 4.3 %copy-start = (bf16[1,272,128]{2,1,0:T(8,128)(2,1)S(1)}, bf16[1,272,128]{2,1,0:T(8,128)(2,1)}, u32[]{:S(2)}) copy-start(bf16[1,272,128]{2,1,0:T(8,128)(2,1)} %pack.1.refs_0_) | copy-start | bytes 208900
  9.2 9.6 %collective-permute-start.3 = (bf16[4,272,128]{2,1,0:T(8,128)(2,1)S(1)}, bf16[4,272,128]{2,1,0:T(8,128)(2,1)S(1)}, u32[]{:S(2)}, u32[]{:S(2)}) collective-permute-start(bf16[4,272,128]{2,1,0:T(8,128)(2,1)S(1)} %join.2.refs_0_), channel_id=1, source_target_pairs={{0,8},{1,9},{2,10},{3,11},{4,12},{5,13},{6,14},{7,15},{8,16},{9,17... | collective-permute-start | bytes 835592 | tf_op jit(solution)/shard_map/ppermute | solution.py:329
  10.6 8.2 %collective-permute-start.4 = (bf16[4,272,128]{2,1,0:T(8,128)(2,1)S(1)}, bf16[4,272,128]{2,1,0:T(8,128)(2,1)S(1)}, u32[]{:S(2)}, u32[]{:S(2)}) collective-permute-start(bf16[4,272,128]{2,1,0:T(8,128)(2,1)S(1)} %join.2.refs_0_), channel_id=1, source_target_pairs={{0,1},{1,0},{2,3},{3,2},{4,5},{5,4},{6,7},{7,6},{8,9},{9,8},{10,11... | collective-permute-start | bytes 835592 | tf_op jit(solution)/shard_map/ppermute | solution.py:329
  13.2 22.5 %collective-permute-start.7 = (bf16[16,128,128]{2,1,0:T(8,128)(2,1)S(1)}, bf16[16,128,128]{2,1,0:T(8,128)(2,1)S(1)}, u32[]{:S(2)}, u32[]{:S(2)}) collective-permute-start(bf16[16,128,128]{2,1,0:T(8,128)(2,1)S(1)} %get-tuple-element.87.own_a), channel_id=1, source_target_pairs={{1,2},{2,4},{3,6},{4,1},{5,3},{6,5},{9,10},{10,12},{11,14},{12,9},... | collective-permute-start | bytes 1572872 | tf_op jit(solution)/shard_map/ppermute | solution.py:329
  15.3 20.5 %collective-permute-start.8 = (bf16[16,128,128]{2,1,0:T(8,128)(2,1)S(1)}, bf16[16,128,128]{2,1,0:T(8,128)(2,1)S(1)}, u32[]{:S(2)}, u32[]{:S(2)}) collective-permute-start(bf16[16,128,128]{2,1,0:T(8,128)(2,1)S(1)} %get-tuple-element.88.own_d), channel_id=1, source_target_pairs={{0,6},{1,4},{3,0},{4,7},{6,3},{7,1},{8,14},{9,12},{11,8},{12,15},{... | collective-permute-start | bytes 1572872 | tf_op jit(solution)/shard_map/ppermute | solution.py:329
  18.8 17.0 %collective-permute-start.9 = (bf16[16,128,128]{2,1,0:T(8,128)(2,1)S(1)}, bf16[16,128,128]{2,1,0:T(8,128)(2,1)S(1)}, u32[]{:S(2)}, u32[]{:S(2)}) collective-permute-start(bf16[16,128,128]{2,1,0:T(8,128)(2,1)S(1)} %get-tuple-element.80), channel_id=1, source_target_pairs={{0,2},{1,0},{2,6},{3,4},{4,3},{5,1},{6,7},{7,5},{8,10},{9,8},{10,1... | collective-permute-start | bytes 1572872 | tf_op jit(solution)/shard_map/ppermute | solution.py:329
  20.2 15.5 %collective-permute-start.5 = (bf16[4,272,128]{2,1,0:T(8,128)(2,1)S(1)}, bf16[4,272,128]{2,1,0:T(8,128)(2,1)S(1)}, u32[]{:S(2)}, u32[]{:S(2)}) collective-permute-start(bf16[4,272,128]{2,1,0:T(8,128)(2,1)S(1)} %join.2.refs_0_), channel_id=1, source_target_pairs={{0,16},{1,17},{2,18},{3,19},{4,20},{5,21},{6,22},{7,23},{8,24},{9,... | collective-permute-start | bytes 835592 | tf_op jit(solution)/shard_map/ppermute | solution.py:329
  21.5 14.1 %collective-permute-start.6 = (bf16[4,272,128]{2,1,0:T(8,128)(2,1)S(1)}, bf16[4,272,128]{2,1,0:T(8,128)(2,1)S(1)}, u32[]{:S(2)}, u32[]{:S(2)}) collective-permute-start(bf16[4,272,128]{2,1,0:T(8,128)(2,1)S(1)} %join.2.refs_0_), channel_id=1, source_target_pairs={{0,24},{1,25},{2,26},{3,27},{4,28},{5,29},{6,30},{7,31},{8,0},{9,1... | collective-permute-start | bytes 835592 | tf_op jit(solution)/shard_map/ppermute | solution.py:329
  35.8 10.6 %collective-permute-start.10 = (bf16[16,272,128]{2,1,0:T(8,128)(2,1)S(1)}, bf16[16,272,128]{2,1,0:T(8,128)(2,1)S(1)}, u32[]{:S(2)}, u32[]{:S(2)}) collective-permute-start(bf16[16,272,128]{2,1,0:T(8,128)(2,1)S(1)} %join.3.lists_mine.amps), channel_id=1, source_target_pairs={{0,1},{1,0},{2,3},{3,2},{4,5},{5,4},{6,7},{7,6},{8,9},{9,8},{10,11... | collective-permute-start | bytes 3342344 | tf_op jit(solution)/shard_map/ppermute | solution.py:329
  36.6 14.0 %collective-permute-start.11 = (bf16[16,128,128]{2,1,0:T(8,128)(2,1)S(1)}, bf16[16,128,128]{2,1,0:T(8,128)(2,1)S(1)}, u32[]{:S(2)}, u32[]{:S(2)}) collective-permute-start(bf16[16,128,128]{2,1,0:T(8,128)(2,1)S(1)} %get-tuple-element.84), channel_id=1, source_target_pairs={{0,4},{1,6},{2,0},{3,2},{4,5},{5,7},{6,1},{7,3},{8,12},{9,14},{10,... | collective-permute-start | bytes 1572872 | tf_op jit(solution)/shard_map/ppermute | solution.py:329
  37.0 23.4 %collective-permute-start.12 = (bf16[16,128,128]{2,1,0:T(8,128)(2,1)S(1)}, bf16[16,128,128]{2,1,0:T(8,128)(2,1)S(1)}, u32[]{:S(2)}, u32[]{:S(2)}) collective-permute-start(bf16[16,128,128]{2,1,0:T(8,128)(2,1)S(1)} %get-tuple-element.90.own_a), channel_id=1, source_target_pairs={{1,2},{2,4},{3,6},{4,1},{5,3},{6,5},{9,10},{10,12},{11,14},{12,9},... | collective-permute-start | bytes 1572872 | tf_op jit(solution)/shard_map/ppermute | solution.py:329
  40.2 22.1 %collective-permute-start.13 = (bf16[16,128,128]{2,1,0:T(8,128)(2,1)S(1)}, bf16[16,128,128]{2,1,0:T(8,128)(2,1)S(1)}, u32[]{:S(2)}, u32[]{:S(2)}) collective-permute-start(bf16[16,128,128]{2,1,0:T(8,128)(2,1)S(1)} %get-tuple-element.92.own_d), channel_id=1, source_target_pairs={{0,6},{1,4},{3,0},{4,7},{6,3},{7,1},{8,14},{9,12},{11,8},{12,15},{... | collective-permute-start | bytes 1572872 | tf_op jit(solution)/shard_map/ppermute | solution.py:329
  51.5 15.8 %collective-permute-start.15 = (bf16[16,128,128]{2,1,0:T(8,128)(2,1)S(1)}, bf16[16,128,128]{2,1,0:T(8,128)(2,1)S(1)}, u32[]{:S(2)}, u32[]{:S(2)}) collective-permute-start(bf16[16,128,128]{2,1,0:T(8,128)(2,1)S(1)} %get-tuple-element.95), channel_id=1, source_target_pairs={{0,1},{1,0},{2,3},{3,2},{4,5},{5,4},{6,7},{7,6},{8,9},{9,8},{10,11... | collective-permute-start | bytes 1572872 | tf_op jit(solution)/shard_map/ppermute | solution.py:329
  52.5 17.8 %collective-permute-start.14 = (bf16[16,128,128]{2,1,0:T(8,128)(2,1)S(1)}, bf16[16,128,128]{2,1,0:T(8,128)(2,1)S(1)}, u32[]{:S(2)}, u32[]{:S(2)}) collective-permute-start(bf16[16,128,128]{2,1,0:T(8,128)(2,1)S(1)} %get-tuple-element.94), channel_id=1, source_target_pairs={{1,8},{3,10},{5,12},{7,14},{8,1},{9,16},{10,3},{11,18},{12,5},{13,... | collective-permute-start | bytes 1572872 | tf_op jit(solution)/shard_map/ppermute | solution.py:329
  60.3 13.0 %collective-permute-start.16 = (bf16[16,128,128]{2,1,0:T(8,128)(2,1)S(1)}, bf16[16,128,128]{2,1,0:T(8,128)(2,1)S(1)}, u32[]{:S(2)}, u32[]{:S(2)}) collective-permute-start(bf16[16,128,128]{2,1,0:T(8,128)(2,1)S(1)} %get-tuple-element.100), channel_id=1, source_target_pairs={{0,2},{1,0},{2,6},{3,4},{4,3},{5,1},{6,7},{7,5},{8,10},{9,8},{10,1... | collective-permute-start | bytes 1572872 | tf_op jit(solution)/shard_map/ppermute | solution.py:329
  60.4 13.7 %collective-permute-start.17 = (bf16[16,128,128]{2,1,0:T(8,128)(2,1)S(1)}, bf16[16,128,128]{2,1,0:T(8,128)(2,1)S(1)}, u32[]{:S(2)}, u32[]{:S(2)}) collective-permute-start(bf16[16,128,128]{2,1,0:T(8,128)(2,1)S(1)} %get-tuple-element.101), channel_id=1, source_target_pairs={{0,4},{1,6},{2,0},{3,2},{4,5},{5,7},{6,1},{7,3},{8,12},{9,14},{10,... | collective-permute-start | bytes 1572872 | tf_op jit(solution)/shard_map/ppermute | solution.py:329
  74.9 9.5 %collective-permute-start.19 = (bf16[16,128,128]{2,1,0:T(8,128)(2,1)S(1)}, bf16[16,128,128]{2,1,0:T(8,128)(2,1)S(1)}, u32[]{:S(2)}, u32[]{:S(2)}) collective-permute-start(bf16[16,128,128]{2,1,0:T(8,128)(2,1)S(1)} %get-tuple-element.109), channel_id=1, source_target_pairs={{0,1},{1,0},{2,3},{3,2},{4,5},{5,4},{6,7},{7,6},{8,9},{9,8},{10,11... | collective-permute-start | bytes 1572872 | tf_op jit(solution)/shard_map/ppermute | solution.py:329
  75.0 12.5 %collective-permute-start.18 = (bf16[16,128,128]{2,1,0:T(8,128)(2,1)S(1)}, bf16[16,128,128]{2,1,0:T(8,128)(2,1)S(1)}, u32[]{:S(2)}, u32[]{:S(2)}) collective-permute-start(bf16[16,128,128]{2,1,0:T(8,128)(2,1)S(1)} %get-tuple-element.108), channel_id=1, source_target_pairs={{1,8},{3,10},{5,12},{7,14},{8,1},{9,16},{10,3},{11,18},{12,5},{13,... | collective-permute-start | bytes 1572872 | tf_op jit(solution)/shard_map/ppermute | solution.py:329
  90.6 8.2 %collective-permute-start.21 = (f32[2,2,128,128]{3,2,1,0:T(8,128)S(1)}, f32[2,2,128,128]{3,2,1,0:T(8,128)S(1)}, u32[]{:S(2)}, u32[]{:S(2)}) collective-permute-start(f32[2,2,128,128]{3,2,1,0:T(8,128)S(1)} %get-tuple-element.118), channel_id=1, source_target_pairs={{0,2},{1,6},{2,0},{3,4},{4,3},{5,7},{6,1},{7,5},{8,10},{9,14},{10,... | collective-permute-start | bytes 786440 | tf_op jit(solution)/shard_map/ppermute | solution.py:329
  90.7 10.0 %collective-permute-start.20 = (f32[2,2,128,128]{3,2,1,0:T(8,128)S(1)}, f32[2,2,128,128]{3,2,1,0:T(8,128)S(1)}, u32[]{:S(2)}, u32[]{:S(2)}) collective-permute-start(f32[2,2,128,128]{3,2,1,0:T(8,128)S(1)} %get-tuple-element.117), channel_id=1, source_target_pairs={{1,4},{3,6},{4,1},{6,3},{9,12},{11,14},{12,9},{14,11},{17,20},{19,... | collective-permute-start | bytes 786440 | tf_op jit(solution)/shard_map/ppermute | solution.py:329
  100.8 1.4 %collective-permute-start.22 = (f32[2,128,128]{2,1,0:T(8,128)S(1)}, f32[2,128,128]{2,1,0:T(8,128)S(1)}, u32[]{:S(2)}, u32[]{:S(2)}) collective-permute-start(f32[2,128,128]{2,1,0:T(8,128)S(1)} %select_bitcast_fusion), channel_id=1, source_target_pairs={{0,1},{1,0},{2,3},{3,2},{4,5},{5,4},{6,7},{7,6},{8,9},{9,8},{10,11... | collective-permute-start | bytes 393224 | tf_op jit(solution)/shard_map/ppermute | solution.py:329

commit v4 on v1

--- a/solution.py
+++ b/solution.py
@@ -270,16 +270,16 @@
 
             @pl.when((owner == 1) | (owner == 2))
             def _():
-                home[k] = inner[owner - 1]
+                home[k] = inner[owner - 1].astype(home.dtype)
 
             @pl.when(owner == last * (QUADS - 1))
             def _():
                 for s in range(nz):
-                    home[k, s] = total(s)
+                    home[k, s] = total(s).astype(home.dtype)
 
             @pl.when(owner == (1 - last) * (QUADS - 1))
             def _():
-                home[k] = beside[...]
+                home[k] = beside[...].astype(home.dtype)
 
 
 def ladder(kind, where, held, outside, weights, nz, before=None, done=()):
@@ -291,7 +291,7 @@
     else:
         kernel = functools.partial(edge_kernel, kind, len(before) > 0)
     if done:
-        shape = [jax.ShapeDtypeStruct((2, nz, w, w), jnp.float32)] * 2
+        shape = [jax.ShapeDtypeStruct((2, nz, w, w), held.dtype)] * 2
     args = [held] + list(outside) + [weights] + before + list(done)
     return pl.pallas_call(
         kernel,
@@ -394,9 +394,10 @@
             held, beyond = lax.optimization_barrier((held, beyond))
 
     stays = (quad >> 1) == core
-    pair = jnp.where(stays, beyond[0], 0.0)
+    pair = jnp.where(stays, beyond[0].astype(jnp.float32), 0.0)
     for v in range(2):
-        pair = pair + send(beyond[v], lambda z, q, k: (z, 2 * k + (v ^ (q & 1)), q >> 1))
+        came = send(beyond[v], lambda z, q, k: (z, 2 * k + (v ^ (q & 1)), q >> 1))
+        pair = pair + came.astype(jnp.float32)
     keep = jnp.where(core == 0, pair[0], pair[1])
     give = jnp.where(core == 0, pair[1], pair[0])
     total = keep + to_core(give)

time: 103 us -> 101 us (0.981)
  waiting for transfers between devices: 29.8 us -> 27.6 us
    ppermute x23, waiting for transfers between devices: 29.8 us -> 27.6 us  [send(): return lax.ppermute(value, 'tile', pairs)]
  transfers between devices with their start and end apart: 23 -> 23, of which waited for: 8 -> 9; matrix products, arithmetic and copies ran while one was open for 3% -> 3% of each run, Pallas kernels for 27% -> 28%
where the time goes in v4:
time: 101 us; the launch traced here: 100 us
  starting transfers between devices  35.4 us (35%)
  Pallas kernels  33.5 us (33%)
  waiting for transfers between devices  27.6 us (27%)
  local copies, waits for them, and re-layouts  2.79 us (3%)
    ppermute x23, starting transfers between devices, send(): return lax.ppermute(value, 'tile', pairs)  35.4 us
    ppermute x23, waiting for transfers between devices, send(): return lax.ppermute(value, 'tile', pairs)  27.6 us
    pallas_call x6, Pallas kernels, ladder(): pl.pallas_call(kernel, out_shape=shape, in_specs=[SMEM] + [VMEM] * len(ar...  22.1 us
    pallas_call x2, Pallas kernels, mix(): pl.pallas_call(functools.partial(mix_kernel, terms, layers), out_shape=se...  8.07 us
    dynamic_slice x1, local copies, waits for them, and re-layouts, cut(): return lax.dynamic_slice_in_dim(factors[0], start, size, axis=0)  2.7 us
  transfers between devices with their start and end apart: 23, of which 9 were waited for; matrix products, arithmetic and copies ran while one was open for 3% of the time, Pallas kernels for 28%

profile of v4, /device:TPU:1, one launch (start us, length us, event | category | flops | bytes accessed | tf_op | source)
XLA Modules:
  0.0 100.3 jit_solution(12140537543252023527)
XLA Ops:
  0.0 1.5 %pack.1.refs_0_ = bf16[1,272,128]{2,1,0:T(8,128)(2,1)} custom-call(bf16[2,128,128]{2,1,0:T(8,128)(2,1)} %refs_0_.1, s32[2,13]{1,0:T(2,128)} %refs_1_.1, s32[2,13]{1,0:T(2,128)} %refs_2_.1, s32[2,13]{1,0:T(2,128)} %refs_3_.1, s32[2,13]{1,0:T(2,128)} %refs_4_.1), custom_call_target="tpu_custom_call" | custom-call | tf_op jit(solution)/shard_map/pack/pallas_call | solution.py:53
  1.5 0.1 stack.23.where
  1.6 2.0 %collective-permute-start = (bf16[1,272,128]{2,1,0:T(8,128)(2,1)}, bf16[1,272,128]{2,1,0:T(8,128)(2,1)S(1)}, u32[]{:S(2)}, u32[]{:S(2)}) collective-permute-start(bf16[1,272,128]{2,1,0:T(8,128)(2,1)} %pack.1.refs_0_), channel_id=1, source_target_pairs={{0,2},{1,3},{2,0},{3,1},{4,6},{5,7},{6,4},{7,5},{8,10},{9,11},{10,... | collective-permute-start | bytes 208904 | tf_op jit(solution)/shard_map/ppermute | solution.py:328
  3.7 1.2 %collective-permute-start.1 = (bf16[1,272,128]{2,1,0:T(8,128)(2,1)}, bf16[1,272,128]{2,1,0:T(8,128)(2,1)S(1)}, u32[]{:S(2)}, u32[]{:S(2)}) collective-permute-start(bf16[1,272,128]{2,1,0:T(8,128)(2,1)} %pack.1.refs_0_), channel_id=1, source_target_pairs={{0,4},{1,5},{2,6},{3,7},{4,0},{5,1},{6,2},{7,3},{8,12},{9,13},{10,... | collective-permute-start | bytes 208904 | tf_op jit(solution)/shard_map/ppermute | solution.py:328
  4.9 0.0 collective-permute-start.2
  4.9 0.0 copy-start
  4.9 2.7 %dynamic-slice_bitcast_fusion = (bf16[16,128,128]{2,1,0:T(8,128)(2,1)S(1)}, bf16[16,128,128]{2,1,0:T(8,128)(2,1)S(1)}, bf16[16,128,128]{2,1,0:T(8,128)(2,1)S(1)}...) fusion(bf16[1,128,128,128]{3,2,1,0:T(8,128)(2,1)} %param.6, ...), kind=kLoop, calls=%fused_computation | loop fusion | bytes 8388640 | tf_op jit(solution)/shard_map/dynamic_slice | solution.py:332
  7.6 0.0 collective-permute-done.refs_1_
  7.6 0.0 collective-permute-done.1.refs_2_
  7.7 1.5 %collective-permute-done.2.refs_3_ = bf16[1,272,128]{2,1,0:T(8,128)(2,1)S(1)} collective-permute-done((bf16[1,272,128]{2,1,0:T(8,128)(2,1)}, bf16[1,272,128]{2,1,0:T(8,128)(2,1)S(1)}, u32[]{:S(2)}, u32[]{:S(2)}) %collective-permute-start.2) | collective-permute-done | bytes 69664 | tf_op jit(solution)/shard_map/ppermute | solution.py:328
  9.2 0.0 copy-done
  9.2 1.3 %collective-permute-start.3 = (bf16[4,272,128]{2,1,0:T(8,128)(2,1)S(1)}, bf16[4,272,128]{2,1,0:T(8,128)(2,1)S(1)}, u32[]{:S(2)}, u32[]{:S(2)}) collective-permute-start(bf16[4,272,128]{2,1,0:T(8,128)(2,1)S(1)} %join.2.refs_0_), channel_id=1, source_target_pairs={{0,8},{1,9},{2,10},{3,11},{4,12},{5,13},{6,14},{7,15},{8,16},{9,17... | collective-permute-start | bytes 835592 | tf_op jit(solution)/shard_map/ppermute | solution.py:328
  10.6 2.6 %collective-permute-start.4 = (bf16[4,272,128]{2,1,0:T(8,128)(2,1)S(1)}, bf16[4,272,128]{2,1,0:T(8,128)(2,1)S(1)}, u32[]{:S(2)}, u32[]{:S(2)}) collective-permute-start(bf16[4,272,128]{2,1,0:T(8,128)(2,1)S(1)} %join.2.refs_0_), channel_id=1, source_target_pairs={{0,1},{1,0},{2,3},{3,2},{4,5},{5,4},{6,7},{7,6},{8,9},{9,8},{10,11... | collective-permute-start | bytes 835592 | tf_op jit(solution)/shard_map/ppermute | solution.py:328
  13.2 2.3 %collective-permute-start.5 = (bf16[4,272,128]{2,1,0:T(8,128)(2,1)S(1)}, bf16[4,272,128]{2,1,0:T(8,128)(2,1)S(1)}, u32[]{:S(2)}, u32[]{:S(2)}) collective-permute-start(bf16[4,272,128]{2,1,0:T(8,128)(2,1)S(1)} %join.2.refs_0_), channel_id=1, source_target_pairs={{0,16},{1,17},{2,18},{3,19},{4,20},{5,21},{6,22},{7,23},{8,24},{9,... | collective-permute-start | bytes 835592 | tf_op jit(solution)/shard_map/ppermute | solution.py:328
  15.5 2.3 %collective-permute-start.10 = (bf16[16,128,128]{2,1,0:T(8,128)(2,1)S(1)}, bf16[16,128,128]{2,1,0:T(8,128)(2,1)S(1)}, u32[]{:S(2)}, u32[]{:S(2)}) collective-permute-start(bf16[16,128,128]{2,1,0:T(8,128)(2,1)S(1)} %get-tuple-element.96.own_d), channel_id=1, source_target_pairs={{0,6},{1,4},{3,0},{4,7},{6,3},{7,1},{8,14},{9,12},{11,8},{12,15},{... | collective-permute-start | bytes 1572872 | tf_op jit(solution)/shard_map/ppermute | solution.py:328
  17.8 1.9 %collective-permute-start.7 = (bf16[16,128,128]{2,1,0:T(8,128)(2,1)S(1)}, bf16[16,128,128]{2,1,0:T(8,128)(2,1)S(1)}, u32[]{:S(2)}, u32[]{:S(2)}) collective-permute-start(bf16[16,128,128]{2,1,0:T(8,128)(2,1)S(1)} %get-tuple-element.95.own_a), channel_id=1, source_target_pairs={{1,2},{2,4},{3,6},{4,1},{5,3},{6,5},{9,10},{10,12},{11,14},{12,9},... | collective-permute-start | bytes 1572872 | tf_op jit(solution)/shard_map/ppermute | solution.py:328
  19.8 0.0 collective-permute-done.3.refs_1_
  19.8 0.0 collective-permute-done.4.lists_other
  19.8 2.5 %collective-permute-start.8 = (bf16[16,128,128]{2,1,0:T(8,128)(2,1)S(1)}, bf16[16,128,128]{2,1,0:T(8,128)(2,1)S(1)}, u32[]{:S(2)}, u32[]{:S(2)}) collective-permute-start(bf16[16,128,128]{2,1,0:T(8,128)(2,1)S(1)} %get-tuple-element.83), channel_id=1, source_target_pairs={{0,2},{1,0},{2,6},{3,4},{4,3},{5,1},{6,7},{7,5},{8,10},{9,8},{10,1... | collective-permute-start | bytes 1572872 | tf_op jit(solution)/shard_map/ppermute | solution.py:328
  22.3 0.8 collective-permute-start.9
  23.1 8.6 %collective-permute-done.5.refs_2_ = bf16[4,272,128]{2,1,0:T(8,128)(2,1)S(1)} collective-permute-done((bf16[4,272,128]{2,1,0:T(8,128)(2,1)S(1)}, bf16[4,272,128]{2,1,0:T(8,128)(2,1)S(1)}, u32[]{:S(2)}, u32[]{:S(2)}) %collective-permute-start.5) | collective-permute-done | bytes 278560 | tf_op jit(solution)/shard_map/ppermute | solution.py:328
  31.7 0.0 collective-permute-start.6
  31.7 7.8 %collective-permute-done.6.refs_3_ = bf16[4,272,128]{2,1,0:T(8,128)(2,1)S(1)} collective-permute-done((bf16[4,272,128]{2,1,0:T(8,128)(2,1)S(1)}, bf16[4,272,128]{2,1,0:T(8,128)(2,1)S(1)}, u32[]{:S(2)}, u32[]{:S(2)}) %collective-permute-start.6) | collective-permute-done | bytes 278560 | tf_op jit(solution)/shard_map/ppermute | solution.py:328
  39.5 0.1 join.3.lists_mine.amps
  39.6 0.0 collective-permute-done.10.d
  39.6 2.1 %collective-permute-done.7.a = bf16[16,128,128]{2,1,0:T(8,128)(2,1)S(1)} collective-permute-done((bf16[16,128,128]{2,1,0:T(8,128)(2,1)S(1)}, bf16[16,128,128]{2,1,0:T(8,128)(2,1)S(1)}, u32[]{:S(2)}, u32[]{:S(2)}) %collective-permute-start.7) | collective-permute-done | bytes 524320 | tf_op jit(solution)/shard_map/ppermute | solution.py:328
  41.7 1.7 %collective-permute-done.8.b = bf16[16,128,128]{2,1,0:T(8,128)(2,1)S(1)} collective-permute-done((bf16[16,128,128]{2,1,0:T(8,128)(2,1)S(1)}, bf16[16,128,128]{2,1,0:T(8,128)(2,1)S(1)}, u32[]{:S(2)}, u32[]{:S(2)}) %collective-permute-start.8) | collective-permute-done | bytes 524320 | tf_op jit(solution)/shard_map/ppermute | solution.py:328
  43.4 0.0 collective-permute-done.9.c
  43.4 0.0 collective-permute-start.14
  43.4 2.0 %collective-permute-start.12 = (bf16[16,128,128]{2,1,0:T(8,128)(2,1)S(1)}, bf16[16,128,128]{2,1,0:T(8,128)(2,1)S(1)}, u32[]{:S(2)}, u32[]{:S(2)}) collective-permute-start(bf16[16,128,128]{2,1,0:T(8,128)(2,1)S(1)} %get-tuple-element.99.own_a), channel_id=1, source_target_pairs={{1,2},{2,4},{3,6},{4,1},{5,3},{6,5},{9,10},{10,12},{11,14},{12,9},... | collective-permute-start | bytes 1572872 | tf_op jit(solution)/shard_map/ppermute | solution.py:328
  45.4 3.9 %mix.2.refs_0_ = f32[4,18,128,128]{3,2,1,0:T(8,128)S(1)} custom-call(s32[6]{0:T(128)S(1)} %stack.23.where, bf16[16,272,128]{2,1,0:T(8,128)(2,1)S(1)} %join.3.lists_mine.amps, bf16[4,272,128]{2,1,0:T(8,128)(2,1)S(1)} %collective-permute-done.4.lists_other, bf16[16,272,128]{2,1,0:T(8,128)(2,1)S(1)} %join.3.lists_mine.amps), custom_call_target="tpu_custom_call" | custom-call | tf_op jit(solution)/shard_map/mix/pallas_call | solution.py:126
  49.3 0.8 sort.2
  50.2 0.1 collective-permute-start.13
  50.2 3.5 %collective-permute-start.15 = (bf16[16,128,128]{2,1,0:T(8,128)(2,1)S(1)}, bf16[16,128,128]{2,1,0:T(8,128)(2,1)S(1)}, u32[]{:S(2)}, u32[]{:S(2)}) collective-permute-start(bf16[16,128,128]{2,1,0:T(8,128)(2,1)S(1)} %get-tuple-element.104.own_d), channel_id=1, source_target_pairs={{0,6},{1,4},{3,0},{4,7},{6,3},{7,1},{8,14},{9,12},{11,8},{12,15},{... | collective-permute-start | bytes 1572872 | tf_op jit(solution)/shard_map/ppermute | solution.py:328
  53.7 2.8 %collective-permute-start.11 = (bf16[16,128,128]{2,1,0:T(8,128)(2,1)S(1)}, bf16[16,128,128]{2,1,0:T(8,128)(2,1)S(1)}, u32[]{:S(2)}, u32[]{:S(2)}) collective-permute-start(bf16[16,128,128]{2,1,0:T(8,128)(2,1)S(1)} %get-tuple-element.97), channel_id=1, source_target_pairs={{1,8},{3,10},{5,12},{7,14},{8,1},{9,16},{10,3},{11,18},{12,5},{13,... | collective-permute-start | bytes 1572872 | tf_op jit(solution)/shard_map/ppermute | solution.py:328
  56.6 0.0 collective-permute-done.12.a
  56.6 0.1 collective-permute-start.16
  56.7 0.0 collective-permute-done.14.lists_other.amps
  56.7 1.5 %collective-permute-start.17 = (bf16[16,128,128]{2,1,0:T(8,128)(2,1)S(1)}, bf16[16,128,128]{2,1,0:T(8,128)(2,1)S(1)}, u32[]{:S(2)}, u32[]{:S(2)}) collective-permute-start(bf16[16,128,128]{2,1,0:T(8,128)(2,1)S(1)} %get-tuple-element.109), channel_id=1, source_target_pairs={{0,4},{1,6},{2,0},{3,2},{4,5},{5,7},{6,1},{7,3},{8,12},{9,14},{10,... | collective-permute-start | bytes 1572872 | tf_op jit(solution)/shard_map/ppermute | solution.py:328
  58.2 4.2 %mix.3.weights = bf16[4,768,384]{2,1,0:T(8,128)(2,1)S(1)} custom-call(s32[6]{0:T(128)S(1)} %stack.23.where, bf16[16,272,128]{2,1,0:T(8,128)(2,1)S(1)} %join.3.lists_mine.amps, bf16[16,272,128]{2,1,0:T(8,128)(2,1)S(1)} %collective-permute-done.14.lists_other.amps, bf16[16,272,128]{2,1,0:T(8,128)(2,1)S(1)} %collective-permute-done.14.lists_other.amps, ...), custom_call_target="tpu_custom_call" | custom-call | tf_op jit(solution)/shard_map/mix/pallas_call | solution.py:126
  62.4 5.0 %inner.2.refs_0_ = f32[2,2,128,128]{3,2,1,0:T(8,128)S(1)} custom-call(s32[6]{0:T(128)S(1)} %stack.23.where, bf16[4,16,128,128]{3,2,1,0:T(8,128)(2,1)S(1)} %get-tuple-element.100.held, bf16[4,768,384]{2,1,0:T(8,128)(2,1)S(1)} %mix.3.weights), custom_call_target="tpu_custom_call" | custom-call | tf_op jit(solution)/shard_map/inner/pallas_call | solution.py:296
  67.4 0.0 collective-permute-done.13.outside
  67.4 0.0 collective-permute-done.15.d
  67.4 3.0 %beside.2.refs_0_ = f32[2,128,128]{2,1,0:T(8,128)S(1)} custom-call(s32[6]{0:T(128)S(1)} %stack.23.where, bf16[4,16,128,128]{3,2,1,0:T(8,128)(2,1)S(1)} %get-tuple-element.100.held, bf16[16,128,128]{2,1,0:T(8,128)(2,1)S(1)} %collective-permute-done.13.outside, bf16[4,768,384]{2,1,0:T(8,128)(2,1)S(1)} %mix.3.weights), custom_call_target="tpu_custom_call" | custom-call | tf_op jit(solution)/shard_map/beside/pallas_call | solution.py:296
  70.5 0.0 collective-permute-done.11.outside
  70.5 1.8 %collective-permute-done.16.b = bf16[16,128,128]{2,1,0:T(8,128)(2,1)S(1)} collective-permute-done((bf16[16,128,128]{2,1,0:T(8,128)(2,1)S(1)}, bf16[16,128,128]{2,1,0:T(8,128)(2,1)S(1)}, u32[]{:S(2)}, u32[]{:S(2)}) %collective-permute-start.16) | collective-permute-done | bytes 524320 | tf_op jit(solution)/shard_map/ppermute | solution.py:328
  72.3 0.0 collective-permute-done.17.c
  72.3 0.8 sort.3
  73.1 0.1 collective-permute-start.19
  73.2 2.5 %collective-permute-start.18 = (bf16[16,128,128]{2,1,0:T(8,128)(2,1)S(1)}, bf16[16,128,128]{2,1,0:T(8,128)(2,1)S(1)}, u32[]{:S(2)}, u32[]{:S(2)}) collective-permute-start(bf16[16,128,128]{2,1,0:T(8,128)(2,1)S(1)} %get-tuple-element.120), channel_id=1, source_target_pairs={{1,8},{3,10},{5,12},{7,14},{8,1},{9,16},{10,3},{11,18},{12,5},{13,... | collective-permute-start | bytes 1572872 | tf_op jit(solution)/shard_map/ppermute | solution.py:328
  75.7 3.0 %beyond.2.refs_0_ = f32[2,128,128]{2,1,0:T(8,128)S(1)} custom-call(s32[6]{0:T(128)S(1)} %stack.23.where, bf16[4,16,128,128]{3,2,1,0:T(8,128)(2,1)S(1)} %get-tuple-element.100.held, bf16[16,128,128]{2,1,0:T(8,128)(2,1)S(1)} %collective-permute-done.11.outside, bf16[4,768,384]{2,1,0:T(8,128)(2,1)S(1)} %mix.3.weights), custom_call_target="tpu_custom_call" | custom-call | tf_op jit(solution)/shard_map/beyond/pallas_call | solution.py:296
  78.8 5.0 %inner.3.refs_1_ = f32[2,2,128,128]{3,2,1,0:T(8,128)S(1)} custom-call(s32[6]{0:T(128)S(1)} %stack.23.where, bf16[4,16,128,128]{3,2,1,0:T(8,128)(2,1)S(1)} %get-tuple-element.119.held, bf16[4,768,384]{2,1,0:T(8,128)(2,1)S(1)} %mix.3.weights, f32[2,2,128,128]{3,2,1,0:T(8,128)S(1)} %inner.2.refs_0_), custom_call_target="tpu_custom_call" | custom-call | tf_op jit(solution)/shard_map/inner/pallas_call | solution.py:296
  83.8 0.0 collective-permute-done.19.outside
  83.8 3.0 %beside.3.refs_2_ = f32[2,128,128]{2,1,0:T(8,128)S(1)} custom-call(s32[6]{0:T(128)S(1)} %stack.23.where, bf16[4,16,128,128]{3,2,1,0:T(8,128)(2,1)S(1)} %get-tuple-element.119.held, bf16[16,128,128]{2,1,0:T(8,128)(2,1)S(1)} %collective-permute-done.19.outside, bf16[4,768,384]{2,1,0:T(8,128)(2,1)S(1)} %mix.3.weights, f32[2,128,128]{2,1,0:T(8,128)S(1)} %beside.2.refs_0_), custom_call_target="tpu_custom_call" | custom-call | tf_op jit(solution)/shard_map/beside/pallas_call | solution.py:296
  86.8 0.0 collective-permute-done.18.outside
  86.8 3.1 %beyond.3 = (bf16[2,2,128,128]{3,2,1,0:T(8,128)(2,1)S(1)}, bf16[2,2,128,128]{3,2,1,0:T(8,128)(2,1)S(1)}) custom-call(s32[6]{0:T(128)S(1)} %stack.23.where, bf16[4,16,128,128]{3,2,1,0:T(8,128)(2,1)S(1)} %get-tuple-element.119.held, bf16[16,128,128]{2,1,0:T(8,128)(2,1)S(1)} %collective-permute-done.18.outside, bf16[4,768,384]{2,1,0:T(8,128)(2,1)S(1)} %mix.3.weights, ...), custom_call_target="tpu_custom_call" | custom-call | tf_op jit(solution)/shard_map/beyond/pallas_call | solution.py:296
  89.9 1.9 %collective-permute-start.20 = (bf16[2,2,128,128]{3,2,1,0:T(8,128)(2,1)S(1)}, bf16[2,2,128,128]{3,2,1,0:T(8,128)(2,1)S(1)}, u32[]{:S(2)}, u32[]{:S(2)}) collective-permute-start(bf16[2,2,128,128]{3,2,1,0:T(8,128)(2,1)S(1)} %get-tuple-element.129), channel_id=1, source_target_pairs={{1,4},{3,6},{4,1},{6,3},{9,12},{11,14},{12,9},{14,11},{17,20},{19,... | collective-permute-start | bytes 393224 | tf_op jit(solution)/shard_map/ppermute | solution.py:328
  91.9 3.6 %collective-permute-start.21 = (bf16[2,2,128,128]{3,2,1,0:T(8,128)(2,1)S(1)}, bf16[2,2,128,128]{3,2,1,0:T(8,128)(2,1)S(1)}, u32[]{:S(2)}, u32[]{:S(2)}) collective-permute-start(bf16[2,2,128,128]{3,2,1,0:T(8,128)(2,1)S(1)} %get-tuple-element.130), channel_id=1, source_target_pairs={{0,2},{1,6},{2,0},{3,4},{4,3},{5,7},{6,1},{7,5},{8,10},{9,14},{10,... | collective-permute-start | bytes 393224 | tf_op jit(solution)/shard_map/ppermute | solution.py:328
  95.5 0.7 collective-permute-done.20
  96.2 1.9 %collective-permute-done.21 = bf16[2,2,128,128]{3,2,1,0:T(8,128)(2,1)S(1)} collective-permute-done((bf16[2,2,128,128]{3,2,1,0:T(8,128)(2,1)S(1)}, bf16[2,2,128,128]{3,2,1,0:T(8,128)(2,1)S(1)}, u32[]{:S(2)}, u32[]{:S(2)}) %collective-permute-start.21) | collective-permute-done | bytes 131104 | tf_op jit(solution)/shard_map/ppermute | solution.py:328
  98.1 0.1 convert_add_fusion
  98.2 0.1 collective-permute-start.22
  98.3 1.3 %collective-permute-done.22 = f32[2,128,128]{2,1,0:T(8,128)S(1)} collective-permute-done((f32[2,128,128]{2,1,0:T(8,128)S(1)}, f32[2,128,128]{2,1,0:T(8,128)S(1)}, u32[]{:S(2)}, u32[]{:S(2)}) %collective-permute-start.22) | collective-permute-done | bytes 131104 | tf_op jit(solution)/shard_map/ppermute | solution.py:328
  99.6 0.7 fusion
  (2 shorter events, 0.0 us)
Async XLA Ops:
  1.6 6.0 %collective-permute-start = (bf16[1,272,128]{2,1,0:T(8,128)(2,1)}, bf16[1,272,128]{2,1,0:T(8,128)(2,1)S(1)}, u32[]{:S(2)}, u32[]{:S(2)}) collective-permute-start(bf16[1,272,128]{2,1,0:T(8,128)(2,1)} %pack.1.refs_0_), channel_id=1, source_target_pairs={{0,2},{1,3},{2,0},{3,1},{4,6},{5,7},{6,4},{7,5},{8,10},{9,11},{10,... | collective-permute-start | bytes 208904 | tf_op jit(solution)/shard_map/ppermute | solution.py:328
  3.7 4.0 %collective-permute-start.1 = (bf16[1,272,128]{2,1,0:T(8,128)(2,1)}, bf16[1,272,128]{2,1,0:T(8,128)(2,1)S(1)}, u32[]{:S(2)}, u32[]{:S(2)}) collective-permute-start(bf16[1,272,128]{2,1,0:T(8,128)(2,1)} %pack.1.refs_0_), channel_id=1, source_target_pairs={{0,4},{1,5},{2,6},{3,7},{4,0},{5,1},{6,2},{7,3},{8,12},{9,13},{10,... | collective-permute-start | bytes 208904 | tf_op jit(solution)/shard_map/ppermute | solution.py:328
  4.9 4.3 %collective-permute-start.2 = (bf16[1,272,128]{2,1,0:T(8,128)(2,1)}, bf16[1,272,128]{2,1,0:T(8,128)(2,1)S(1)}, u32[]{:S(2)}, u32[]{:S(2)}) collective-permute-start(bf16[1,272,128]{2,1,0:T(8,128)(2,1)} %pack.1.refs_0_), channel_id=1, source_target_pairs={{0,6},{1,7},{2,4},{3,5},{4,2},{5,3},{6,0},{7,1},{8,14},{9,15},{10,... | collective-permute-start | bytes 208904 | tf_op jit(solution)/shard_map/ppermute | solution.py:328
  4.9 4.3 %copy-start = (bf16[1,272,128]{2,1,0:T(8,128)(2,1)S(1)}, bf16[1,272,128]{2,1,0:T(8,128)(2,1)}, u32[]{:S(2)}) copy-start(bf16[1,272,128]{2,1,0:T(8,128)(2,1)} %pack.1.refs_0_) | copy-start | bytes 208900
  9.2 10.5 %collective-permute-start.3 = (bf16[4,272,128]{2,1,0:T(8,128)(2,1)S(1)}, bf16[4,272,128]{2,1,0:T(8,128)(2,1)S(1)}, u32[]{:S(2)}, u32[]{:S(2)}) collective-permute-start(bf16[4,272,128]{2,1,0:T(8,128)(2,1)S(1)} %join.2.refs_0_), channel_id=1, source_target_pairs={{0,8},{1,9},{2,10},{3,11},{4,12},{5,13},{6,14},{7,15},{8,16},{9,17... | collective-permute-start | bytes 835592 | tf_op jit(solution)/shard_map/ppermute | solution.py:328
  10.6 9.2 %collective-permute-start.4 = (bf16[4,272,128]{2,1,0:T(8,128)(2,1)S(1)}, bf16[4,272,128]{2,1,0:T(8,128)(2,1)S(1)}, u32[]{:S(2)}, u32[]{:S(2)}) collective-permute-start(bf16[4,272,128]{2,1,0:T(8,128)(2,1)S(1)} %join.2.refs_0_), channel_id=1, source_target_pairs={{0,1},{1,0},{2,3},{3,2},{4,5},{5,4},{6,7},{7,6},{8,9},{9,8},{10,11... | collective-permute-start | bytes 835592 | tf_op jit(solution)/shard_map/ppermute | solution.py:328
  13.2 18.5 %collective-permute-start.5 = (bf16[4,272,128]{2,1,0:T(8,128)(2,1)S(1)}, bf16[4,272,128]{2,1,0:T(8,128)(2,1)S(1)}, u32[]{:S(2)}, u32[]{:S(2)}) collective-permute-start(bf16[4,272,128]{2,1,0:T(8,128)(2,1)S(1)} %join.2.refs_0_), channel_id=1, source_target_pairs={{0,16},{1,17},{2,18},{3,19},{4,20},{5,21},{6,22},{7,23},{8,24},{9,... | collective-permute-start | bytes 835592 | tf_op jit(solution)/shard_map/ppermute | solution.py:328
  15.5 24.1 %collective-permute-start.10 = (bf16[16,128,128]{2,1,0:T(8,128)(2,1)S(1)}, bf16[16,128,128]{2,1,0:T(8,128)(2,1)S(1)}, u32[]{:S(2)}, u32[]{:S(2)}) collective-permute-start(bf16[16,128,128]{2,1,0:T(8,128)(2,1)S(1)} %get-tuple-element.96.own_d), channel_id=1, source_target_pairs={{0,6},{1,4},{3,0},{4,7},{6,3},{7,1},{8,14},{9,12},{11,8},{12,15},{... | collective-permute-start | bytes 1572872 | tf_op jit(solution)/shard_map/ppermute | solution.py:328
  17.8 23.9 %collective-permute-start.7 = (bf16[16,128,128]{2,1,0:T(8,128)(2,1)S(1)}, bf16[16,128,128]{2,1,0:T(8,128)(2,1)S(1)}, u32[]{:S(2)}, u32[]{:S(2)}) collective-permute-start(bf16[16,128,128]{2,1,0:T(8,128)(2,1)S(1)} %get-tuple-element.95.own_a), channel_id=1, source_target_pairs={{1,2},{2,4},{3,6},{4,1},{5,3},{6,5},{9,10},{10,12},{11,14},{12,9},... | collective-permute-start | bytes 1572872 | tf_op jit(solution)/shard_map/ppermute | solution.py:328
  19.8 23.6 %collective-permute-start.8 = (bf16[16,128,128]{2,1,0:T(8,128)(2,1)S(1)}, bf16[16,128,128]{2,1,0:T(8,128)(2,1)S(1)}, u32[]{:S(2)}, u32[]{:S(2)}) collective-permute-start(bf16[16,128,128]{2,1,0:T(8,128)(2,1)S(1)} %get-tuple-element.83), channel_id=1, source_target_pairs={{0,2},{1,0},{2,6},{3,4},{4,3},{5,1},{6,7},{7,5},{8,10},{9,8},{10,1... | collective-permute-start | bytes 1572872 | tf_op jit(solution)/shard_map/ppermute | solution.py:328
  22.3 21.1 %collective-permute-start.9 = (bf16[16,128,128]{2,1,0:T(8,128)(2,1)S(1)}, bf16[16,128,128]{2,1,0:T(8,128)(2,1)S(1)}, u32[]{:S(2)}, u32[]{:S(2)}) collective-permute-start(bf16[16,128,128]{2,1,0:T(8,128)(2,1)S(1)} %get-tuple-element.84), channel_id=1, source_target_pairs={{0,4},{1,6},{2,0},{3,2},{4,5},{5,7},{6,1},{7,3},{8,12},{9,14},{10,... | collective-permute-start | bytes 1572872 | tf_op jit(solution)/shard_map/ppermute | solution.py:328
  31.7 7.8 %collective-permute-start.6 = (bf16[4,272,128]{2,1,0:T(8,128)(2,1)S(1)}, bf16[4,272,128]{2,1,0:T(8,128)(2,1)S(1)}, u32[]{:S(2)}, u32[]{:S(2)}) collective-permute-start(bf16[4,272,128]{2,1,0:T(8,128)(2,1)S(1)} %join.2.refs_0_), channel_id=1, source_target_pairs={{0,24},{1,25},{2,26},{3,27},{4,28},{5,29},{6,30},{7,31},{8,0},{9,1... | collective-permute-start | bytes 835592 | tf_op jit(solution)/shard_map/ppermute | solution.py:328
  43.4 13.3 %collective-permute-start.14 = (bf16[16,272,128]{2,1,0:T(8,128)(2,1)S(1)}, bf16[16,272,128]{2,1,0:T(8,128)(2,1)S(1)}, u32[]{:S(2)}, u32[]{:S(2)}) collective-permute-start(bf16[16,272,128]{2,1,0:T(8,128)(2,1)S(1)} %join.3.lists_mine.amps), channel_id=1, source_target_pairs={{0,1},{1,0},{2,3},{3,2},{4,5},{5,4},{6,7},{7,6},{8,9},{9,8},{10,11... | collective-permute-start | bytes 3342344 | tf_op jit(solution)/shard_map/ppermute | solution.py:328
  43.4 13.2 %collective-permute-start.12 = (bf16[16,128,128]{2,1,0:T(8,128)(2,1)S(1)}, bf16[16,128,128]{2,1,0:T(8,128)(2,1)S(1)}, u32[]{:S(2)}, u32[]{:S(2)}) collective-permute-start(bf16[16,128,128]{2,1,0:T(8,128)(2,1)S(1)} %get-tuple-element.99.own_a), channel_id=1, source_target_pairs={{1,2},{2,4},{3,6},{4,1},{5,3},{6,5},{9,10},{10,12},{11,14},{12,9},... | collective-permute-start | bytes 1572872 | tf_op jit(solution)/shard_map/ppermute | solution.py:328
  50.2 17.3 %collective-permute-start.13 = (bf16[16,128,128]{2,1,0:T(8,128)(2,1)S(1)}, bf16[16,128,128]{2,1,0:T(8,128)(2,1)S(1)}, u32[]{:S(2)}, u32[]{:S(2)}) collective-permute-start(bf16[16,128,128]{2,1,0:T(8,128)(2,1)S(1)} %get-tuple-element.101), channel_id=1, source_target_pairs={{0,1},{1,0},{2,3},{3,2},{4,5},{5,4},{6,7},{7,6},{8,9},{9,8},{10,11... | collective-permute-start | bytes 1572872 | tf_op jit(solution)/shard_map/ppermute | solution.py:328
  50.2 17.2 %collective-permute-start.15 = (bf16[16,128,128]{2,1,0:T(8,128)(2,1)S(1)}, bf16[16,128,128]{2,1,0:T(8,128)(2,1)S(1)}, u32[]{:S(2)}, u32[]{:S(2)}) collective-permute-start(bf16[16,128,128]{2,1,0:T(8,128)(2,1)S(1)} %get-tuple-element.104.own_d), channel_id=1, source_target_pairs={{0,6},{1,4},{3,0},{4,7},{6,3},{7,1},{8,14},{9,12},{11,8},{12,15},{... | collective-permute-start | bytes 1572872 | tf_op jit(solution)/shard_map/ppermute | solution.py:328
  53.7 16.7 %collective-permute-start.11 = (bf16[16,128,128]{2,1,0:T(8,128)(2,1)S(1)}, bf16[16,128,128]{2,1,0:T(8,128)(2,1)S(1)}, u32[]{:S(2)}, u32[]{:S(2)}) collective-permute-start(bf16[16,128,128]{2,1,0:T(8,128)(2,1)S(1)} %get-tuple-element.97), channel_id=1, source_target_pairs={{1,8},{3,10},{5,12},{7,14},{8,1},{9,16},{10,3},{11,18},{12,5},{13,... | collective-permute-start | bytes 1572872 | tf_op jit(solution)/shard_map/ppermute | solution.py:328
  56.6 15.7 %collective-permute-start.16 = (bf16[16,128,128]{2,1,0:T(8,128)(2,1)S(1)}, bf16[16,128,128]{2,1,0:T(8,128)(2,1)S(1)}, u32[]{:S(2)}, u32[]{:S(2)}) collective-permute-start(bf16[16,128,128]{2,1,0:T(8,128)(2,1)S(1)} %get-tuple-element.108), channel_id=1, source_target_pairs={{0,2},{1,0},{2,6},{3,4},{4,3},{5,1},{6,7},{7,5},{8,10},{9,8},{10,1... | collective-permute-start | bytes 1572872 | tf_op jit(solution)/shard_map/ppermute | solution.py:328
  56.7 15.6 %collective-permute-start.17 = (bf16[16,128,128]{2,1,0:T(8,128)(2,1)S(1)}, bf16[16,128,128]{2,1,0:T(8,128)(2,1)S(1)}, u32[]{:S(2)}, u32[]{:S(2)}) collective-permute-start(bf16[16,128,128]{2,1,0:T(8,128)(2,1)S(1)} %get-tuple-element.109), channel_id=1, source_target_pairs={{0,4},{1,6},{2,0},{3,2},{4,5},{5,7},{6,1},{7,3},{8,12},{9,14},{10,... | collective-permute-start | bytes 1572872 | tf_op jit(solution)/shard_map/ppermute | solution.py:328
  73.1 10.6 %collective-permute-start.19 = (bf16[16,128,128]{2,1,0:T(8,128)(2,1)S(1)}, bf16[16,128,128]{2,1,0:T(8,128)(2,1)S(1)}, u32[]{:S(2)}, u32[]{:S(2)}) collective-permute-start(bf16[16,128,128]{2,1,0:T(8,128)(2,1)S(1)} %get-tuple-element.121), channel_id=1, source_target_pairs={{0,1},{1,0},{2,3},{3,2},{4,5},{5,4},{6,7},{7,6},{8,9},{9,8},{10,11... | collective-permute-start | bytes 1572872 | tf_op jit(solution)/shard_map/ppermute | solution.py:328
  73.2 13.6 %collective-permute-start.18 = (bf16[16,128,128]{2,1,0:T(8,128)(2,1)S(1)}, bf16[16,128,128]{2,1,0:T(8,128)(2,1)S(1)}, u32[]{:S(2)}, u32[]{:S(2)}) collective-permute-start(bf16[16,128,128]{2,1,0:T(8,128)(2,1)S(1)} %get-tuple-element.120), channel_id=1, source_target_pairs={{1,8},{3,10},{5,12},{7,14},{8,1},{9,16},{10,3},{11,18},{12,5},{13,... | collective-permute-start | bytes 1572872 | tf_op jit(solution)/shard_map/ppermute | solution.py:328
  89.9 6.3 %collective-permute-start.20 = (bf16[2,2,128,128]{3,2,1,0:T(8,128)(2,1)S(1)}, bf16[2,2,128,128]{3,2,1,0:T(8,128)(2,1)S(1)}, u32[]{:S(2)}, u32[]{:S(2)}) collective-permute-start(bf16[2,2,128,128]{3,2,1,0:T(8,128)(2,1)S(1)} %get-tuple-element.129), channel_id=1, source_target_pairs={{1,4},{3,6},{4,1},{6,3},{9,12},{11,14},{12,9},{14,11},{17,20},{19,... | collective-permute-start | bytes 393224 | tf_op jit(solution)/shard_map/ppermute | solution.py:328
  91.9 6.3 %collective-permute-start.21 = (bf16[2,2,128,128]{3,2,1,0:T(8,128)(2,1)S(1)}, bf16[2,2,128,128]{3,2,1,0:T(8,128)(2,1)S(1)}, u32[]{:S(2)}, u32[]{:S(2)}) collective-permute-start(bf16[2,2,128,128]{3,2,1,0:T(8,128)(2,1)S(1)} %get-tuple-element.130), channel_id=1, source_target_pairs={{0,2},{1,6},{2,0},{3,4},{4,3},{5,7},{6,1},{7,5},{8,10},{9,14},{10,... | collective-permute-start | bytes 393224 | tf_op jit(solution)/shard_map/ppermute | solution.py:328
  98.2 1.4 %collective-permute-start.22 = (f32[2,128,128]{2,1,0:T(8,128)S(1)}, f32[2,128,128]{2,1,0:T(8,128)S(1)}, u32[]{:S(2)}, u32[]{:S(2)}) collective-permute-start(f32[2,128,128]{2,1,0:T(8,128)S(1)} %select_bitcast_fusion), channel_id=1, source_target_pairs={{0,1},{1,0},{2,3},{3,2},{4,5},{5,4},{6,7},{7,6},{8,9},{9,8},{10,11... | collective-permute-start | bytes 393224 | tf_op jit(solution)/shard_map/ppermute | solution.py:328
